TPU v7x, 128 devices: a whole 4x4x4 slice. The times are simulated.
128 devices in a mesh: seq: 8 (over y, core), own: 16 (over x, z).
Axes of the slice: x: 4, y: 4, z: 4, core: 2. Of those that a mesh axis runs over, the one named last changes fastest.
Arguments:
- d_out: bfloat16 [32, 2048, 512], P('own', 'seq'), may hold values from -6 to 6
- weight_in: bfloat16 [512, 2048], replicated, may hold values from -0.25 to 0.25
- weight_out: bfloat16 [512, 512], replicated, may hold values from -0.25 to 0.25
- hot_table: bfloat16 [512, 512], replicated, may hold values from -6 to 6
- cold_table: bfloat16 [262144, 512], P(('seq', 'own')), may hold values from -6 to 6
- cold_ids: int32 [16384, 4], P(('seq', 'own')), may hold values from 0 to 2047
- cold_counts: int32 [16384], P(('seq', 'own')), may hold values from 2 to 4
- event_slots: int32 [32, 2048], P('own', 'seq'), may hold values from 0 to 1023, as said below
- lengths: int32 [32], P('own'), may hold values from 512 to 2048, as said below
Outputs:
- grad_w_in: float32 [512, 2048], replicated
- grad_w_out: float32 [512, 512], replicated
- hot_grad: float32 [512, 512], replicated
- cold_grad: float32 [262144, 512], P(('seq', 'own'))
Inputs may be any that keep to these rules, and one draw needn't show every extreme that they name: `cold_ids`: row ids inside one owner's shard. `event_slots`: a position at or above 512 names a valid slot of the request rows of the device that holds it. `lengths`: some user has all 2048 events in every draw.
All inputs are finite; a program needn't handle non-finite values.
Results may differ from a plain program's by a relative error of at most 0.0065.
Values may be sent and summed in bfloat16 or wider, within the bound.
A program may use at most 192 MiB of HBM per device.

v0:
```python
import jax
import jax.numpy as jnp
from jax import lax
from jax.sharding import PartitionSpec as P

HEAD_DIM = 128


def silu_slope(values):
    sigma = jax.nn.sigmoid(values)
    return sigma * (1.0 + values * (1.0 - sigma))


def split_heads(block, head_size):
    return block.reshape(block.shape[:-1] + (block.shape[-1] // head_size, head_size))


def attend_mask(query_pos, key_pos, lengths):
    causal = key_pos[None, :] <= query_pos[:, None]
    present = key_pos[None, None, :] < lengths[:, None, None]
    return (causal[None] & present).astype(jnp.float32)[:, None]


def on_device(
    d_out, weight_in, weight_out, hot_table, cold_table, cold_ids, cold_counts, event_slots, lengths
):
    seq_count = lax.axis_size("seq")
    own_count = lax.axis_size("own")
    dev_count = seq_count * own_count
    users, seq_len = event_slots.shape
    width = weight_out.shape[0]
    slots = cold_ids.shape[1]
    hot_rows = hot_table.shape[0]
    full_len = seq_len * seq_count
    scale = HEAD_DIM ** (-0.5)
    asked = lax.all_to_all(cold_ids, ("seq", "own"), split_axis=0, concat_axis=0, tiled=True)
    fetched = lax.all_to_all(
        cold_table[asked], ("seq", "own"), split_axis=0, concat_axis=0, tiled=True
    )
    valid = jnp.arange(slots, dtype=jnp.int32)[None, :] < cold_counts[:, None]
    fetched = jnp.where(valid[:, :, None], fetched, jnp.zeros((), fetched.dtype)).reshape(
        dev_count * slots, width
    )
    is_hot = event_slots < hot_rows
    hot_index = jnp.clip(event_slots, 0, hot_rows - 1)
    cold_index = jnp.clip(event_slots - hot_rows, 0, dev_count * slots - 1)
    embedded = jnp.where(is_hot[..., None], hot_table[hot_index], fetched[cold_index])
    positions = lax.axis_index("seq") * seq_len + jnp.arange(seq_len, dtype=jnp.int32)
    all_pos = jnp.arange(full_len, dtype=jnp.int32)
    live_rows = positions[None, :] < lengths[:, None]
    cotangent = jnp.where(live_rows[..., None], d_out, jnp.zeros((), d_out.dtype))
    inv_len = (1.0 / lengths.astype(jnp.float32))[:, None, None, None]
    hidden_pre = jnp.einsum("utd,df->utf", embedded, weight_in, preferred_element_type=jnp.float32)
    projected = jax.nn.silu(hidden_pre).astype(jnp.bfloat16)
    gate_part = projected[..., :width].astype(jnp.float32)
    query_part = projected[..., width : 2 * width]
    keyval_local = projected[..., 2 * width :]
    keyval_all = lax.all_gather(keyval_local, "seq", axis=1, tiled=True)
    query_heads = split_heads(query_part, HEAD_DIM)
    key_heads = split_heads(keyval_all[..., :width], HEAD_DIM)
    value_heads = split_heads(keyval_all[..., width:], HEAD_DIM)
    mask_here = attend_mask(positions, all_pos, lengths)
    scores = (
        jnp.einsum("uthd,ushd->uhts", query_heads, key_heads, preferred_element_type=jnp.float32)
        * scale
    )
    weights = (jax.nn.silu(scores) * mask_here * inv_len).astype(jnp.bfloat16)
    attended = jnp.einsum(
        "uhts,ushd->uthd", weights, value_heads, preferred_element_type=jnp.float32
    ).reshape(users, seq_len, width)
    centered = attended - jnp.mean(attended, axis=-1, keepdims=True)
    rstd = lax.rsqrt(jnp.mean(centered * centered, axis=-1, keepdims=True) + 1e-05)
    normed = centered * rstd
    gated = (normed * gate_part).astype(jnp.bfloat16)
    grad_w_out = jnp.einsum("uti,utj->ij", gated, cotangent, preferred_element_type=jnp.float32)
    grad_gated = jnp.einsum(
        "utj,ij->uti", cotangent, weight_out, preferred_element_type=jnp.float32
    )
    grad_gate = grad_gated * normed
    grad_normed = grad_gated * gate_part
    grad_att = (
        (
            grad_normed
            - jnp.mean(grad_normed, axis=-1, keepdims=True)
            - normed * jnp.mean(grad_normed * normed, axis=-1, keepdims=True)
        )
        * rstd
    ).astype(jnp.bfloat16)
    grad_heads = split_heads(grad_att, HEAD_DIM)
    grad_weights = jnp.einsum(
        "uthd,ushd->uhts", grad_heads, value_heads, preferred_element_type=jnp.float32
    )
    grad_scores = (grad_weights * silu_slope(scores) * mask_here * inv_len).astype(jnp.bfloat16)
    grad_query = (
        jnp.einsum("uhts,ushd->uthd", grad_scores, key_heads, preferred_element_type=jnp.float32)
        * scale
    )
    grad_key = (
        jnp.einsum("uhts,uthd->ushd", grad_scores, query_heads, preferred_element_type=jnp.float32)
        * scale
    )
    grad_val = jnp.einsum(
        "uhts,uthd->ushd", weights, grad_heads, preferred_element_type=jnp.float32
    )
    partial_kv = jnp.concatenate(
        [grad_key.reshape(users, full_len, width), grad_val.reshape(users, full_len, width)],
        axis=-1,
    )
    grad_keyval = lax.psum_scatter(partial_kv, "seq", scatter_dimension=1, tiled=True)
    grad_proj = jnp.concatenate(
        [grad_gate, grad_query.reshape(users, seq_len, width), grad_keyval], axis=-1
    )
    grad_hidden = (grad_proj * silu_slope(hidden_pre)).astype(jnp.bfloat16)
    grad_w_in = jnp.einsum("utd,utf->df", embedded, grad_hidden, preferred_element_type=jnp.float32)
    grad_embed = jnp.einsum(
        "utf,df->utd", grad_hidden, weight_in, preferred_element_type=jnp.float32
    ) + cotangent.astype(jnp.float32)
    flat = grad_embed.reshape(-1, width)
    hot_flag = is_hot.reshape(-1, 1)
    hot_sum = jax.ops.segment_sum(
        jnp.where(hot_flag, flat, 0.0), hot_index.reshape(-1), num_segments=hot_rows
    )
    slot_sum = jax.ops.segment_sum(
        jnp.where(hot_flag, 0.0, flat), cold_index.reshape(-1), num_segments=dev_count * slots
    )
    slot_sum = jnp.where(valid[:, :, None], slot_sum.reshape(dev_count, slots, width), 0.0)
    returned = lax.all_to_all(slot_sum, ("seq", "own"), split_axis=0, concat_axis=0, tiled=True)
    cold_grad = jax.ops.segment_sum(
        returned.reshape(-1, width), asked.reshape(-1), num_segments=cold_table.shape[0]
    )
    summed = lax.psum((grad_w_in, grad_w_out, hot_sum), ("seq", "own"))
    return (summed[0], summed[1], summed[2], cold_grad)


def solution(mesh):
    placed = (
        P("own", "seq", None),
        P(),
        P(),
        P(),
        P(("seq", "own"), None),
        P(("seq", "own"), None),
        P(("seq", "own")),
        P("own", "seq"),
        P("own"),
    )
    return jax.shard_map(
        on_device,
        mesh=mesh,
        in_specs=placed,
        out_specs=(P(), P(), P(), P(("seq", "own"), None)),
        check_vma=False,
    )
```

profile of v0, /device:TPU:1, one launch (start us, length us, event | category | flops | bytes accessed | tf_op | source)
XLA Modules:
  0.0 498.0 jit_solution(12233189660711592217)
XLA Ops:
  8.7 11.5 %all-to-all-start = ((s32[128,1,4]{2,1,0:T(1,128)}), s32[128,1,4]{2,1,0:T(1,128)S(1)}, u32[]{:S(2)}, u32[]{:S(2)}) async-start(s32[128,1,4]{2,1,0:T(1,128)} %bitcast.1), calls=%async_computation | async-start | bytes 131072 | tf_op jit(solution)/shard_map/all_to_all | solution.py:36
  21.0 3.1 gather_fusion
  25.1 4.6 all-to-all-done
  29.8 3.8 gather_fusion.1
  34.6 5.2 %all-to-all-start.1 = ((bf16[128,4,512]{2,1,0:T(4,128)(2,1)}), bf16[128,4,512]{2,1,0:T(4,128)(2,1)S(1)}, u32[]{:S(2)}, u32[]{:S(2)}) async-start(bf16[128,4,512]{2,1,0:T(4,128)(2,1)} %reshape.219), calls=%async_computation.1 | async-start | bytes 1048576 | tf_op jit(solution)/shard_map/all_to_all | solution.py:37
  40.0 13.2 %all-to-all-done.1 = bf16[128,4,512]{2,1,0:T(4,128)(2,1)S(1)} async-done(((bf16[128,4,512]{2,1,0:T(4,128)(2,1)}), bf16[128,4,512]{2,1,0:T(4,128)(2,1)S(1)}, u32[]{:S(2)}, u32[]{:S(2)}) %all-to-all-start.1) | async-done | bytes 524320 | tf_op jit(solution)/shard_map/all_to_all | solution.py:37
  55.9 5.1 %multiply_convert_fusion.2 = (bf16[2,256,2048]{2,1,0:T(8,128)(2,1)S(1)}, f32[2,256,2048]{2,1,0:T(8,128)}) fusion(bf16[512,2048]{1,0:T(8,128)(2,1)S(1)} %copy-done, bf16[2,256,512]{1,2,0:T(8,128)(2,1)} %copy.48, bf16[2,256,512]{1,2,0:T(8,128)(2,1)S(1)} %copy.49, pred[2,256]{1,0:T(4,128)(4,1)S(1)} %broadcast_compare_fusion.1), kind=kOutput, calls=%fused_computation.17 | convolution fusion | flops 1079246848 | bytes 9437696 | tf_op jit(solution)/shard_map/utd,df->utf/dot_general | solution.py:53
  64.0 2.6 and_convert_fusion
  67.9 42.2 %all-gather.2.cloned.1.call-done = bf16[2,2048,1024]{2,1,0:T(8,128)(2,1)} async-done(((bf16[2,256,1024]{2,1,0:T(8,128)(2,1)}), bf16[2,2048,1024]{2,1,0:T(8,128)(2,1)}) %all-gather.2.cloned.1.call-update) | async-done | bytes 8388624 | tf_op jit(solution)/shard_map/all_gather | solution.py:58
  110.0 6.0 %slice_bitcast_fusion = (bf16[2,256,4,8,128]{4,3,2,1,0:T(8,128)(2,1)}, bf16[2,2048,512]{2,1,0:T(8,128)(2,1)}) fusion(bf16[2,2048,1024]{2,1,0:T(8,128)(2,1)} %all-gather.2.cloned.1.call-done), kind=kLoop, calls=%fused_computation.14 | loop fusion | bytes 16777216
  116.1 6.3 %copy.71 = bf16[2,2048,512]{1,2,0:T(8,128)(2,1)} copy(bf16[2,2048,512]{2,1,0:T(8,128)(2,1)} %get-tuple-element.10) | data formatting | bytes 8388608 | tf_op jit(solution)/shard_map/reshape | solution.py:15
  122.3 13.0 %multiply_convert_fusion.1 = (bf16[2,4,256,2048]{3,2,1,0:T(8,128)(2,1)S(1)}, f32[2,4,256,2048]{3,2,1,0:T(8,128)}) fusion(f32[2]{0:T(128)S(1)} %convert_divide_fusion, f32[2,256,2048]{2,1,0:T(8,128)} %and_convert_fusion, bf16[2,256,4,128]{1,3,2,0:T(8,128)(2,1)S(1)} %bitcast.87, bf16[2,2048,4,128]{1,3,2,0:T(8,128)(2,1)} %bitcast.83), kind=kOutput, calls=%fused_computation.8 | convolution fusion | flops 1107296256 | bytes 34078728 | tf_op jit(solution)/shard_map/uthd,ushd->uhts/dot_general | solution.py:64
  135.4 8.1 %bitcast_reduce_fusion = (f32[2,256]{1,0:T(2,128)S(1)}, f32[2,4,128,256]{3,2,1,0:T(8,128)S(1)}) fusion(bf16[2,4,256,2048]{3,2,1,0:T(8,128)(2,1)S(1)} %get-tuple-element.21, bf16[2,256,4,8,128]{4,3,2,1,0:T(8,128)(2,1)} %get-tuple-element.9), kind=kOutput, calls=%fused_computation.38 | convolution fusion | flops 1074003456 | bytes 13633536 | tf_op jit(solution)/shard_map/uhts,ushd->uthd/dot_general | solution.py:68
  150.9 8.2 %fusion.37 = f32[2,4,128,2048]{3,2,1,0:T(8,128)} fusion(bf16[2,256,4,128]{1,3,2,0:T(8,128)(2,1)} %bitcast.89, bf16[2,4,256,2048]{3,2,1,0:T(8,128)(2,1)} %copy-done.1), kind=kOutput, calls=%fused_computation.85 | convolution fusion | flops 1073741824 | bytes 17301504 | tf_op jit(solution)/shard_map/uhts,uthd->ushd/dot_general | solution.py:102
  159.2 14.4 %multiply_convert_fusion = bf16[2,4,256,2048]{3,2,1,0:T(8,128)(2,1)} fusion(f32[2,4,256,2048]{3,2,1,0:T(8,128)} %get-tuple-element.22, f32[2]{0:T(128)S(1)} %convert_divide_fusion, f32[2,256,2048]{2,1,0:T(8,128)} %and_convert_fusion, bf16[2,256,4,128]{1,3,2,0:T(8,128)(2,1)} %bitcast.90, bf16[2,256,4,8,128]{4,3,2,1,0:T(8,128)(2,1)S(1)} %copy-done.2), kind=kOutput, calls=%fused_computation.7 | convolution fusion | flops 1124073472 | bytes 34078728 | tf_op jit(solution)/shard_map/uthd,ushd->uhts/dot_general | solution.py:90
  173.6 8.4 %convolution_multiply_fusion = f32[2,4,128,2048]{3,2,1,0:T(8,128)} fusion(bf16[2,256,4,128]{1,3,2,0:T(8,128)(2,1)} %bitcast.88, bf16[2,4,256,2048]{3,2,1,0:T(8,128)(2,1)} %multiply_convert_fusion), kind=kOutput, calls=%fused_computation.10 | convolution fusion | flops 1075838976 | bytes 17301504 | tf_op jit(solution)/shard_map/uhts,uthd->ushd/dot_general | solution.py:99
  182.0 8.7 %copy.69 = f32[2,2048,512]{2,1,0:T(8,128)} copy(f32[2,2048,512]{1,2,0:T(8,128)} %bitcast.81) | data formatting | bytes 16777216 | tf_op jit(solution)/shard_map/reshape | solution.py:106
  190.7 8.7 %copy.68 = f32[2,2048,512]{2,1,0:T(8,128)} copy(f32[2,2048,512]{1,2,0:T(8,128)} %bitcast.82) | data formatting | bytes 16777216 | tf_op jit(solution)/shard_map/reshape | solution.py:106
  199.4 11.7 %pad_maximum_fusion = f32[2,2048,1024]{2,1,0:T(8,128)} fusion(f32[2,2048,512]{2,1,0:T(8,128)} %copy.69, f32[2,2048,512]{2,1,0:T(8,128)} %copy.68), kind=kLoop, calls=%fused_computation.6 | loop fusion | flops 4194304 | bytes 33554432 | tf_op jit(solution)/shard_map/concatenate | solution.py:105
  211.2 8.6 %convolution_multiply_fusion.1 = f32[2,4,128,256]{3,2,1,0:T(8,128)} fusion(bf16[2,2048,4,128]{1,3,2,0:T(8,128)(2,1)} %bitcast.84, bf16[2,4,256,2048]{3,2,1,0:T(8,128)(2,1)} %multiply_convert_fusion), kind=kOutput, calls=%fused_computation.31 | convolution fusion | flops 1074003968 | bytes 13631488 | tf_op jit(solution)/shard_map/uhts,ushd->uthd/dot_general | solution.py:95
  221.5 3.2 convolution_bitcast_fusion.1
  224.8 77.5 %reduce-scatter.2.cloned.1.call-done = f32[2,256,1024]{2,1,0:T(8,128)} async-done(((f32[2,2048,1024]{2,1,0:T(8,128)}), f32[2,256,1024]{2,1,0:T(8,128)}) %reduce-scatter.2.cloned.1.call-update) | async-done | bytes 2097168 | tf_op jit(solution)/shard_map/reduce_scatter | solution.py:109
  302.2 4.0 fusion.3
  307.7 3.3 convolution_bitcast_fusion
  312.1 4.6 scatter_custom_fusion
  316.8 4.8 scatter_custom_fusion.1
  322.8 2.5 broadcast_select_fusion
  325.3 8.4 %all-to-all-start.2 = ((f32[128,4,512]{2,1,0:T(4,128)}), f32[128,4,512]{2,1,0:T(4,128)S(1)}, u32[]{:S(2)}, u32[]{:S(2)}) async-start(f32[128,4,512]{2,1,0:T(4,128)} %broadcast_select_fusion), calls=%async_computation.3 | async-start | bytes 2097152 | tf_op jit(solution)/shard_map/all_to_all | solution.py:127
  335.1 19.6 %all-to-all-done.2 = f32[128,4,512]{2,1,0:T(4,128)S(1)} async-done(((f32[128,4,512]{2,1,0:T(4,128)}), f32[128,4,512]{2,1,0:T(4,128)S(1)}, u32[]{:S(2)}, u32[]{:S(2)}) %all-to-all-start.2) | async-done | bytes 1048608 | tf_op jit(solution)/shard_map/all_to_all | solution.py:127
  356.1 6.5 %scatter_custom_fusion.2 = f32[2048,512]{1,0:T(8,128)} fusion(s32[512]{0:T(512)S(1)} %reshape.252, f32[512,512]{1,0:T(8,128)} %reshape.254, f32[]{:T(128)} %constant.11.clone.1), kind=kCustom, calls=%fused_computation.27 | custom fusion | flops 262144 | bytes 4194816 | tf_op jit(solution)/shard_map/scatter-add | solution.py:128
  362.6 121.7 %all-reduce.3.cloned.1.call-done = (f32[512,2048]{1,0:T(8,128)}, f32[512,512]{1,0:T(8,128)}, f32[512,512]{1,0:T(8,128)}) async-done(((f32[512,2048]{1,0:T(8,128)}, f32[512,512]{1,0:T(8,128)}, f32[512,512]{1,0:T(8,128)}), (f32[512,2048]{1,0:T(8,128)}, f32[512,512]{1,0:T(8,128)}, f32[512,512]{1,0:T(8,128)})) %all-reduce.3.cloned.1.call-update) | async-done | bytes 6291472 | tf_op jit(solution)/shard_map/psum | solution.py:131
  484.3 4.8 copy.91
  (82 shorter events, 29.1 us)
Async XLA Ops:
  7.2 48.7 %copy-start = (bf16[512,2048]{1,0:T(8,128)(2,1)S(1)}, bf16[512,2048]{1,0:T(8,128)(2,1)}, u32[]{:S(2)}) copy-start(bf16[512,2048]{1,0:T(8,128)(2,1)} %param.10) | copy-start | bytes 6291460
  8.7 21.0 %all-to-all-start = ((s32[128,1,4]{2,1,0:T(1,128)}), s32[128,1,4]{2,1,0:T(1,128)S(1)}, u32[]{:S(2)}, u32[]{:S(2)}) async-start(s32[128,1,4]{2,1,0:T(1,128)} %bitcast.1), calls=%async_computation | async-start | bytes 131072 | tf_op jit(solution)/shard_map/all_to_all | solution.py:36
  24.1 15.8 %copy-start.11 = (s32[2,256]{1,0:T(2,128)S(1)}, s32[2,256]{1,0:T(2,128)}, u32[]{:S(2)}) copy-start(s32[2,256]{1,0:T(2,128)} %param.16) | copy-start | bytes 6148
  24.1 15.8 %copy-start.13 = (s32[128]{0:T(128)S(1)}, s32[128]{0:T(128)}, u32[]{:S(2)}) copy-start(s32[128]{0:T(128)} %param.15) | copy-start | bytes 1540
  34.6 18.6 %all-to-all-start.1 = ((bf16[128,4,512]{2,1,0:T(4,128)(2,1)}), bf16[128,4,512]{2,1,0:T(4,128)(2,1)S(1)}, u32[]{:S(2)}, u32[]{:S(2)}) async-start(bf16[128,4,512]{2,1,0:T(4,128)(2,1)} %reshape.219), calls=%async_computation.1 | async-start | bytes 1048576 | tf_op jit(solution)/shard_map/all_to_all | solution.py:37
  39.8 70.3 %all-gather.2.cloned.1.call-start = ((), (), s32[]{:S(2)}) async-start(), calls=%async_computation.4 | async-start | bytes 9437184 | tf_op jit(solution)/shard_map/all_gather | solution.py:58
  55.9 5.1 %copy-start.7 = (bf16[2,256,512]{1,2,0:T(8,128)(2,1)}, bf16[2,256,512]{1,2,0:T(8,128)(2,1)S(1)}, u32[]{:S(2)}) copy-start(bf16[2,256,512]{1,2,0:T(8,128)(2,1)S(1)} %copy.49) | copy-start | bytes 1572868
  55.9 7.6 %copy-start.12 = (s32[2]{0:T(128)S(1)}, s32[2]{0:T(128)}, u32[]{:S(2)}) copy-start(s32[2]{0:T(128)} %param.17) | copy-start | bytes 28
  61.0 1.3 copy-start.5
  63.4 238.8 %reduce-scatter.2.cloned.1.call-start = ((), (), s32[]{:S(2)}) async-start(), calls=%async_computation.5 | async-start | bytes 18874368 | tf_op jit(solution)/shard_map/reduce_scatter | solution.py:109
  67.9 54.5 %copy-start.4 = (bf16[2,256,512]{1,2,0:T(8,128)(2,1)}, bf16[2,256,512]{1,2,0:T(8,128)(2,1)S(1)}, u32[]{:S(2)}) copy-start(bf16[2,256,512]{1,2,0:T(8,128)(2,1)S(1)} %copy.70) | copy-start | bytes 1572868
  135.4 8.2 %copy-start.1 = (bf16[2,4,256,2048]{3,2,1,0:T(8,128)(2,1)}, bf16[2,4,256,2048]{3,2,1,0:T(8,128)(2,1)S(1)}, u32[]{:S(2)}) copy-start(bf16[2,4,256,2048]{3,2,1,0:T(8,128)(2,1)S(1)} %get-tuple-element.21) | copy-start | bytes 25165828
  145.0 2.5 copy-start.3
  150.9 8.2 %copy-start.2 = (bf16[2,256,4,8,128]{4,3,2,1,0:T(8,128)(2,1)S(1)}, bf16[2,256,4,8,128]{4,3,2,1,0:T(8,128)(2,1)}, u32[]{:S(2)}) copy-start(bf16[2,256,4,8,128]{4,3,2,1,0:T(8,128)(2,1)} %get-tuple-element.9) | copy-start | bytes 12582916
  211.2 273.1 %all-reduce.3.cloned.1.call-start = ((), (), s32[]{:S(2)}) async-start(), calls=%async_computation.6 | async-start | bytes 12582912 | tf_op jit(solution)/shard_map/psum | solution.py:131
  302.2 4.0 copy-start.14
  306.2 1.4 copy-start.6
  306.2 1.4 copy-start.8
  325.3 29.4 %all-to-all-start.2 = ((f32[128,4,512]{2,1,0:T(4,128)}), f32[128,4,512]{2,1,0:T(4,128)S(1)}, u32[]{:S(2)}, u32[]{:S(2)}) async-start(f32[128,4,512]{2,1,0:T(4,128)} %broadcast_select_fusion), calls=%async_computation.3 | async-start | bytes 2097152 | tf_op jit(solution)/shard_map/all_to_all | solution.py:127
  484.3 4.9 copy-start.10
  484.3 5.8 %copy-start.9 = (f32[512,512]{1,0:T(8,128)S(1)}, f32[512,512]{1,0:T(8,128)}, u32[]{:S(2)}) copy-start(f32[512,512]{1,0:T(8,128)} %get-tuple-element.30) | copy-start | bytes 3145732
Sparse Core Ops, SparseCore 0:
  63.5 46.4 all-gather.1
  211.3 90.8 reduce-scatter.1
  316.9 167.3 all-reduce.2
where the time goes:
time: 505 us; the launch traced here: 498 us
  waiting for transfers between devices  279 us (55%)
  matrix products  76.3 us (15%)
  local copies, waits for them, and re-layouts  60.3 us (12%)
  other arithmetic  42.9 us (8%)
  starting transfers between devices  25.1 us (5%)
  between operations  14.6 us (3%)
    psum x1, waiting for transfers between devices, on_device(): summed = lax.psum((grad_w_in, grad_w_out, hot_sum), ('seq', 'own'))  122 us
    reduce_scatter x1, waiting for transfers between devices, on_device(): lax.psum_scatter(partial_kv, 'seq', scatter_dimension=1, tiled=True)  77.5 us
    all_gather x1, waiting for transfers between devices, on_device(): keyval_all = lax.all_gather(keyval_local, 'seq', axis=1, tiled=True)  42.2 us
    all_to_all x1, waiting for transfers between devices, on_device(): lax.all_to_all(slot_sum, ('seq', 'own'), split_axis=0, concat_axis=0, til...  19.6 us
    unnamed x39, local copies, waits for them, and re-layouts  15.8 us
    dot_general x1, matrix products, on_device(): jnp.einsum('uthd,ushd->uhts', grad_heads, value_heads, preferred_element_...  14.4 us
    all_to_all x1, waiting for transfers between devices, on_device(): lax.all_to_all(cold_table[asked], ('seq', 'own'), split_axis=0, concat_ax...  13.2 us
    dot_general x1, matrix products, on_device(): jnp.einsum('uthd,ushd->uhts', query_heads, key_heads, preferred_element_t...  13 us
  transfers between devices with their start and end apart: 6, of which 6 were waited for; matrix products, arithmetic and copies ran while one was open for 8% of the time, Pallas kernels for 0%

commit v1 on v0

v1 whole, which is shorter than its diff:
```python
import functools

import jax
import jax.numpy as jnp
from jax import lax
from jax.experimental import pallas as pl
from jax.experimental.pallas import tpu as pltpu
from jax.sharding import PartitionSpec as P

F32 = jnp.float32
BF16 = jnp.bfloat16
MESH = pl.DeviceIdType.MESH
SCALE = 128 ** (-0.5)
AG_ORDERS = (("z", "x", "y"), ("x", "y", "z"), ("y", "z", "x"))
AG_WIDTHS = (256, 256, 128)


def mm(a, b):
    return jnp.dot(a, b, preferred_element_type=F32)


def mm_nt(a, b):
    return lax.dot_general(a, b, (((1,), (1,)), ((), ())), preferred_element_type=F32)


def iota(shape, dim):
    return lax.broadcasted_iota(jnp.int32, shape, dim)


class Exchange:
    def __init__(self, n, me, device, src, dst, send_sem, recv_sem):
        self.n, self.me, self.device, self.src, self.dst = n, me, device, src, dst
        self.send_sem, self.recv_sem = send_sem, recv_sem

    def _out(self, p):
        return pltpu.make_async_remote_copy(
            src_ref=self.src(p),
            dst_ref=self.dst(self.me),
            send_sem=self.send_sem.at[p],
            recv_sem=self.recv_sem.at[self.me],
            device_id=self.device(p),
            device_id_type=MESH,
        )

    def _in(self, p):
        return pltpu.make_async_remote_copy(
            src_ref=self.src(p),
            dst_ref=self.dst(p),
            send_sem=self.send_sem.at[p],
            recv_sem=self.recv_sem.at[p],
            device_id=self.device(p),
            device_id_type=MESH,
        )

    def peer(self, k):
        return lax.rem(self.me + k, self.n)

    def _each(self, f):
        if self.n <= 4:
            for k in range(1, self.n):
                f(self.peer(k))
        else:
            pl.loop(1, self.n)(lambda k: f(self.peer(k)))

    def start(self):
        self._each(lambda p: self._out(p).start())

    def wait_recv(self):
        self._each(lambda p: self._in(p).wait_recv())

    def wait_send(self):
        self._each(lambda p: self._out(p).wait_send())


def main_kernel(
    ids_ref, code_col, code_row, valid_row, valid_col, len_ref, inv_ref, dout_ref, wout_ref, hot_ref, table_ref,
    win_ref,
    agw0, agw1, agw2, agh, ret, asked,
    id_a, id_b, got, rows, perm, fetched, e_loc, e_all, c_all,
    wh, wht, wh_sem, slope_pre, u_t, q_t, k_t, v_t, q_n, k_n, v_n,
    w_st, sl_st, att, gg, gat, ga_t, ga_n, gq, gk, gv, g_t,
    stat1, stat2, sib_s, sib_r, y_s, y_r, grad, w_send, w_recv, wu_s, wu_r, h_send, h_recv, hu_s, hu_r,
    s_send, q_recv, p_send,
    sem16, sem8, sem4, sem_ag, sem_sib,
):
    s, o = lax.axis_index("seq"), lax.axis_index("own")
    y, c = s // 2, lax.rem(s, 2)
    u, h = s // 4, lax.rem(s, 4)
    x, z = o // 4, lax.rem(o, 4)
    sib = (2 * y + 1 - c, o)
    agws = (agw0, agw1, agw2)

    barrier = pltpu.get_barrier_semaphore()

    @pl.loop(1, 16)
    def _(k):
        pl.semaphore_signal(barrier, inc=1, device_id=(s, lax.rem(o + k, 16)), device_id_type=MESH)

    @pl.loop(1, 8)
    def _(k):
        pl.semaphore_signal(barrier, inc=1, device_id=(lax.rem(s + k, 8), o), device_id_type=MESH)

    def load_w(b):
        return pltpu.make_async_copy(
            win_ref.at[:, pl.ds(pl.multiple_of(b * 512 + h * 128, 128), 128)],
            wh.at[:, pl.ds(b * 128, 128)],
            wh_sem.at[b],
        )

    for b in range(4):
        load_w(b).start()

    def own_x(i, src, dst):
        return Exchange(16, o, lambda p: (s, p), src, dst, sem16.at[i, 0], sem16.at[i, 1])

    def seq_x(i, src, dst):
        return Exchange(8, s, lambda p: (p, o), src, dst, sem8.at[i, 0], sem8.at[i, 1])

    def y_x(i, src, dst):
        return Exchange(4, y, lambda p: (2 * p + c, o), src, dst, sem4.at[i, 0], sem4.at[i, 1])

    def head_x(i, src, dst):
        return Exchange(4, h, lambda p: (4 * u + p, o), src, dst, sem4.at[i, 0], sem4.at[i, 1])

    def to_sib(src, dst, ssem, rsem):
        return pltpu.make_async_remote_copy(
            src_ref=src, dst_ref=dst, send_sem=ssem, recv_sem=rsem, device_id=sib, device_id_type=MESH
        )

    ids_x1 = own_x(0, lambda p: ids_ref.at[p], lambda p: id_a.at[p])
    ids_x2 = seq_x(0, lambda p: id_a.at[:, p], lambda p: id_b.at[p])
    rows_x1 = seq_x(1, lambda p: got.at[:, p], lambda p: rows.at[p])
    rows_x2 = own_x(1, lambda p: perm.at[p], lambda p: fetched.at[p])
    cot_x = y_x(0, lambda p: dout_ref.at[p // 2], lambda p: c_all.at[2 * p + c])
    emb_x = y_x(1, lambda p: e_loc.at[p // 2], lambda p: e_all.at[2 * p + c])
    stat1_x = head_x(2, lambda p: stat1.at[h], lambda p: stat1.at[p])
    stat2_x = head_x(3, lambda p: stat2.at[h], lambda p: stat2.at[p])
    grad_x = y_x(4, lambda p: y_s.at[p], lambda p: y_r.at[p])
    w_x = own_x(2, lambda p: w_send.at[p], lambda p: w_recv.at[p])
    hot_x1 = own_x(3, lambda p: h_send.at[p], lambda p: h_recv.at[p])
    hot_x2 = seq_x(2, lambda p: hu_s.at[p], lambda p: hu_r.at[p])
    ret_x1 = own_x(4, lambda p: s_send.at[p], lambda p: q_recv.at[p])
    ret_x2 = seq_x(3, lambda p: p_send.at[p], lambda p: ret.at[:, p])

    def sib_block(buf, i, yy):
        blk = buf.at[2 * yy + c]
        return to_sib(blk, blk, sem_sib.at[i, 0, yy], sem_sib.at[i, 1, yy])

    def sib_block_in(buf, i, yy):
        blk = buf.at[2 * yy + 1 - c]
        return to_sib(blk, blk, sem_sib.at[i, 0, yy], sem_sib.at[i, 1, yy])

    pl.semaphore_wait(barrier, 22)

    ids_x1.start()
    id_a[o] = ids_ref[o]
    cot_x.start()
    c_all[s] = dout_ref[u]
    sib_block(c_all, 0, y).start()
    for b in range(4):
        load_w(b).wait()
    wht[...] = wh[...].T
    ids_x1.wait_recv()
    ids_x2.start()
    id_b[s] = id_a[:, s, :]
    ids_x2.wait_recv()

    asked_ids = id_b[...].reshape(128, 128)
    for i in range(4):
        onehot = (iota((128, 2048), 1) == asked_ids[:, i : i + 1]).astype(F32).astype(BF16)
        got[i] = mm(onehot, table_ref[...]).astype(BF16).reshape(8, 16, 512)
    rows_x1.start()
    rows[s] = got[:, s]
    asked[...] = asked_ids.T[0:8, :]
    for d in (1, 3, 2):
        yy = lax.rem(y + d, 4)
        cot_x._in(yy).wait_recv()
        sib_block(c_all, 0, yy).start()
    rows_x1.wait_recv()
    r = iota((512, 512), 0)
    pick = (iota((512, 512), 1) == lax.rem(r, 32) * 16 + r // 32).astype(F32).astype(BF16)
    perm[...] = mm(pick, rows[...].reshape(512, 512)).astype(BF16).reshape(16, 32, 512)
    rows_x2.start()
    fetched[o] = perm[o]
    emb = []
    for b in range(4):
        hit = (code_col[...] == iota((512, 128), 1) + b * 128).astype(F32).astype(BF16)
        part = mm(hit, hot_ref[b * 128 : (b + 1) * 128, :])
        emb = part if b == 0 else emb + part
    rows_x2.wait_recv()
    for b in range(4):
        ok = jnp.logical_and(
            code_col[...] == iota((512, 128), 1) + (512 + b * 128), valid_row[:, b * 128 : (b + 1) * 128] > 0
        )
        emb += mm(ok.astype(F32).astype(BF16), fetched[4 * b : 4 * b + 4].reshape(128, 512))
    e_loc[...] = emb.astype(BF16).reshape(2, 256, 512)
    emb_x.start()
    e_all[s] = e_loc[u]
    sib_block(e_all, 1, y).start()

    def project(blk):
        cols = pl.ds(pl.multiple_of(blk * 256, 256), 256)
        pre = mm_nt(wht[...], e_all[blk])
        sig = 0.5 + 0.5 * jnp.tanh(0.5 * pre)
        act = pre * sig
        slope_pre[:, cols] = sig + act * (1.0 - sig)
        act = act.astype(BF16)
        u_t[:, cols] = act[0:128]
        q_t[:, cols] = act[128:256]
        k_t[:, cols] = act[256:384]
        keep = (blk * 256 + iota((1, 256), 1) < len_ref[u]).astype(F32)
        val = (act[384:512].astype(F32) * keep).astype(BF16)
        v_t[:, cols] = val
        q_n[cols, :] = act[128:256].T
        k_n[cols, :] = act[256:384].T
        v_n[cols, :] = val.T

    project(s)
    for d in (1, 3, 2):
        yy = lax.rem(y + d, 4)
        emb_x._in(yy).wait_recv()
        sib_block(e_all, 1, yy).start()
        project(2 * yy + c)
    for d in (0, 1, 3, 2):
        yy = lax.rem(y + d, 4)
        sib_block_in(e_all, 1, yy).wait_recv()
        project(2 * yy + 1 - c)

    att[...] = jnp.zeros_like(att)

    def forward(i, j, diag):
        keys = pl.multiple_of(j * 512, 512)
        qs = pl.ds(pl.multiple_of(i * 512, 512), 512)
        at = i * (i + 1) // 2 + j
        for m in range(4):
            half = mm(k_n[pl.ds(keys + m * 128, 128), :], q_t[:, qs]) * (0.5 * SCALE)
            t = jnp.tanh(half)
            a = 1.0 + t
            w = half * a
            slope = a * ((1.0 + 2.0 * half) - w)
            if diag:
                ok = iota((128, 512), 0) + m * 128 <= iota((128, 512), 1)
                w = jnp.where(ok, w, 0.0)
                slope = jnp.where(ok, slope, 0.0)
            w_st[at, m * 128 : (m + 1) * 128, :] = w.astype(BF16)
            sl_st[at, m * 128 : (m + 1) * 128, :] = slope.astype(BF16)
        att[:, qs] += mm(v_t[:, pl.ds(keys, 512)], w_st[at])

    @pl.loop(0, 4)
    def _(i):
        @pl.loop(0, i)
        def _(j):
            forward(i, j, False)

        forward(i, i, True)

    inv = inv_ref[u]
    mine = att[...] * inv
    m1 = jnp.sum(mine, axis=0, keepdims=True) * (1.0 / 128)
    dev = mine - m1
    stat1[h, 0:1, :] = m1
    stat1[h, 1:2, :] = jnp.sum(dev * dev, axis=0, keepdims=True)
    stat1_x.start()
    for d in range(4):
        sib_block_in(c_all, 0, lax.rem(y + d, 4)).wait_recv()
    live = (iota((1, 2048), 1) < len_ref[u]).astype(F32)
    wo = wout_ref[pl.ds(pl.multiple_of(h * 128, 128), 128), :]
    gg[...] = mm_nt(wo, c_all[...].reshape(2048, 512)) * live
    stat1_x.wait_recv()
    all1 = stat1[...]
    mean = jnp.sum(all1[:, 0, :], axis=0, keepdims=True) * 0.25
    off = all1[:, 0, :] - mean
    var = (jnp.sum(all1[:, 1, :], axis=0, keepdims=True) + 128.0 * jnp.sum(off * off, axis=0, keepdims=True)) * (
        1.0 / 512
    )
    rstd = lax.rsqrt(var + 1e-05)
    normed = (att[...] * inv - mean) * rstd
    att[...] = normed
    gate = u_t[...].astype(F32)
    gn = gg[...] * gate
    stat2[h, 0:1, :] = jnp.sum(gn, axis=0, keepdims=True)
    stat2[h, 1:2, :] = jnp.sum(gn * normed, axis=0, keepdims=True)
    stat2_x.start()
    gat[...] = (normed * gate * live).astype(BF16)
    gw_out = mm(gat[...], c_all[...].reshape(2048, 512))
    for b in range(4):
        w_send[4 * b : 4 * b + 4, :, 512:640] = gw_out[:, b * 128 : (b + 1) * 128].astype(BF16).reshape(4, 32, 128)
    g_t[0:128, :] = (gg[...] * att[...] * slope_pre[0:128, :]).astype(BF16)
    stat2_x.wait_recv()
    all2 = stat2[...]
    mean1 = jnp.sum(all2[:, 0, :], axis=0, keepdims=True) * (1.0 / 512)
    mean2 = jnp.sum(all2[:, 1, :], axis=0, keepdims=True) * (1.0 / 512)
    ga = (gg[...] * u_t[...].astype(F32) - mean1 - att[...] * mean2) * (rstd * inv)
    ga_t[...] = ga.astype(BF16)
    for b in range(8):
        ga_n[b * 256 : (b + 1) * 256, :] = ga_t[:, b * 256 : (b + 1) * 256].T

    gq[...] = jnp.zeros_like(gq)
    gk[...] = jnp.zeros_like(gk)
    gv[...] = jnp.zeros_like(gv)

    def backward(i, j):
        keys = pl.multiple_of(j * 512, 512)
        qs = pl.ds(pl.multiple_of(i * 512, 512), 512)
        at = i * (i + 1) // 2 + j
        for m in range(4):
            gw = mm(v_n[pl.ds(keys + m * 128, 128), :], ga_t[:, qs])
            ds = gw * sl_st[at, m * 128 : (m + 1) * 128, :].astype(F32)
            sl_st[at, m * 128 : (m + 1) * 128, :] = ds.astype(BF16)
        gk[pl.ds(keys, 512), :] += mm(sl_st[at], q_n[qs, :])
        gv[pl.ds(keys, 512), :] += mm(w_st[at], ga_n[qs, :])
        gq[:, qs] += mm(k_t[:, pl.ds(keys, 512)], sl_st[at])

    @pl.loop(0, 4)
    def _(i):
        @pl.loop(0, i + 1)
        def _(j):
            backward(i, j)

    keep = (iota((1, 2048), 1) < len_ref[u]).astype(F32)
    g_t[128:256, :] = (gq[...] * (0.5 * SCALE) * slope_pre[128:256, :]).astype(BF16)
    for b in range(8):
        cols = slice(b * 256, (b + 1) * 256)
        g_t[256:384, cols] = (gk[cols, :].T * (0.5 * SCALE) * slope_pre[256:384, cols]).astype(BF16)
        g_t[384:512, cols] = (gv[cols, :].T * keep[:, cols] * slope_pre[384:512, cols]).astype(BF16)

    def partial(blk):
        return mm(wh[...], g_t[:, pl.ds(pl.multiple_of(blk * 256, 256), 256)])

    def sib_grad(yy):
        return to_sib(sib_s.at[yy], sib_r.at[yy], sem_sib.at[2, 0, yy], sem_sib.at[2, 1, yy])

    for d in (2, 1, 3, 0):
        yy = lax.rem(y + d, 4)
        sib_s[yy] = partial(2 * yy + 1 - c).astype(BF16)
        sib_grad(yy).start()
    for d in (2, 1, 3, 0):
        yy = lax.rem(y + d, 4)
        total = partial(2 * yy + c)
        sib_grad(yy).wait_recv()
        total = (total + sib_r[yy].astype(F32)).astype(BF16)
        if d == 0:
            y_r[yy] = total
        else:
            y_s[yy] = total
            grad_x._out(yy).start()

    gw_in = mm(g_t[...], e_all[...].reshape(2048, 512))
    w_send[:, :, 0:512] = gw_in.T.astype(BF16).reshape(16, 32, 512)
    w_x.start()
    w_recv[o] = w_send[o]

    grad_x.wait_recv()
    for uu in range(2):
        grad[:, uu * 256 : (uu + 1) * 256] = (y_r[2 * uu].astype(F32) + y_r[2 * uu + 1].astype(F32)).astype(BF16)
    cots = []
    for uu in range(2):
        here = (s * 256 + iota((256, 1), 0) < len_ref[uu]).astype(F32)
        cots.append((dout_ref[uu].astype(F32) * here).astype(BF16))
    cot = jnp.concatenate(cots, axis=0)
    for b in (1, 0):
        blocks = []
        for l in range(4):
            hit = iota((512, 128), 0) + b * 512 == code_row[:, l * 128 : (l + 1) * 128]
            if b == 1:
                hit = jnp.logical_and(hit, valid_col[...] > 0)
            blocks.append(hit.astype(F32).astype(BF16))
        onehot = jnp.concatenate(blocks, axis=1)
        sums = (mm_nt(onehot, grad[...]) + mm(onehot, cot)).astype(BF16).reshape(16, 32, 512)
        if b == 1:
            s_send[...] = sums
            ret_x1.start()
            q_recv[o] = s_send[o]
        else:
            h_send[...] = sums
            hot_x1.start()
            h_recv[o] = h_send[o]

    w_x.wait_recv()
    total = jnp.sum(w_recv[...].astype(F32), axis=0)
    wu_s[...] = total.astype(BF16).reshape(2, 16, 640)
    partner = (lax.rem(s + 4, 8), o)
    wu = pltpu.make_async_remote_copy(
        src_ref=wu_s.at[1 - u],
        dst_ref=wu_r,
        send_sem=sem_sib.at[3, 0, 0],
        recv_sem=sem_sib.at[3, 1, 0],
        device_id=partner,
        device_id_type=MESH,
    )
    wu.start()

    place = {"y": y, "x": x, "z": z}
    device = {
        "y": lambda p: (2 * p + c, o),
        "x": lambda p: (s, 4 * p + z),
        "z": lambda p: (s, 4 * x + p),
    }

    def gather_x(buf, i, order, stage):
        axis = order[stage]

        def block(p):
            at = dict(place)
            at[axis] = p
            for done in order[:stage]:
                at[done] = slice(None)
            return buf.at[c, at["y"], at["x"], at["z"]]

        return Exchange(
            4, place[axis], device[axis], lambda p: block(place[axis]), block,
            sem_ag.at[i, stage, 0], sem_ag.at[i, stage, 1],
        )

    def sib_gather(buf, i, core):
        return to_sib(buf.at[core], buf.at[core], sem_sib.at[4, 0, i], sem_sib.at[4, 1, i])

    w_gathers = [[gather_x(agws[i], i, AG_ORDERS[i], stage) for stage in range(3)] for i in range(3)]
    h_gather = [gather_x(agh, 3, AG_ORDERS[0], stage) for stage in range(3)]

    ret_x1.wait_recv()
    r = iota((512, 512), 0)
    pick = (iota((512, 512), 1) == lax.rem(r, 16) * 32 + r // 16).astype(F32).astype(BF16)
    p_send[...] = mm(pick, q_recv[...].reshape(512, 512)).astype(BF16).reshape(8, 4, 16, 512)
    ret_x2.start()
    ret[:, s] = p_send[s]

    wu.wait_recv()
    mine = (total[0:16] * (1.0 - u.astype(F32)) + total[16:32] * u.astype(F32)) + wu_r[...].astype(F32)
    mine = mine.astype(BF16)
    agw0[c, y, x, z] = mine[:, 0:256]
    agw1[c, y, x, z] = mine[:, 256:512]
    agw2[c, y, x, z] = mine[:, 512:640]
    for i in range(3):
        w_gathers[i][0].start()

    hot_x1.wait_recv()
    total = jnp.sum(h_recv[...].astype(F32), axis=0).astype(BF16)
    for i in range(8):
        hu_s[i] = total[16 * (i // 4) : 16 * (i // 4) + 16, 128 * (i % 4) : 128 * (i % 4) + 128]
    hot_x2.start()
    hu_r[s] = hu_s[s]

    for i in range(3):
        w_gathers[i][0].wait_recv()
        w_gathers[i][1].start()
    hot_x2.wait_recv()
    agh[c, y, x, z] = jnp.sum(hu_r[...].astype(F32), axis=0).astype(BF16)
    h_gather[0].start()
    for i in range(3):
        w_gathers[i][1].wait_recv()
        w_gathers[i][2].start()
    h_gather[0].wait_recv()
    h_gather[1].start()
    h_gather[1].wait_recv()
    h_gather[2].start()
    for i in range(3):
        w_gathers[i][2].wait_recv()
        sib_gather(agws[i], i, c).start()
    h_gather[2].wait_recv()
    sib_gather(agh, 3, c).start()
    ret_x2.wait_recv()
    for i in range(4):
        sib_gather((*agws, agh)[i], i, 1 - c).wait_recv()

    for step in (ids_x1, ids_x2, rows_x1, rows_x2, cot_x, emb_x, stat1_x, stat2_x, grad_x, w_x):
        step.wait_send()
    for step in (hot_x1, hot_x2, ret_x1, ret_x2, *h_gather, *w_gathers[0], *w_gathers[1], *w_gathers[2]):
        step.wait_send()
    for yy in range(4):
        sib_block(c_all, 0, yy).wait_send()
        sib_block(e_all, 1, yy).wait_send()
        sib_grad(yy).wait_send()
    wu.wait_send()
    for i in range(4):
        sib_gather((*agws, agh)[i], i, c).wait_send()


def finish_kernel(a0, a1, a2, ah, ret, asked, gin, gout, ghot, gcold):
    g = pl.program_id(0)
    for yy in range(4):
        for core in range(2):
            user, head = yy // 2, (yy % 2) * 2 + core
            seq = 2 * yy + core
            for zz in range(2):
                top = 32 * zz + 16 * user
                b0 = a0[core, yy, 0, zz].astype(F32)
                b1 = a1[core, yy, 0, zz].astype(F32)
                for b in range(4):
                    part = (b0, b1)[b // 2][:, (b % 2) * 128 : (b % 2) * 128 + 128]
                    gin[top : top + 16, b * 512 + head * 128 : b * 512 + head * 128 + 128] = part
                low = pl.multiple_of(head * 128 + 32 * (2 * lax.rem(g, 2) + zz) + 16 * user, 16)
                gout[pl.ds(low, 16), pl.ds(pl.multiple_of(g // 2 * 128, 128), 128)] = a2[core, yy, 0, zz].astype(F32)
                hot_top = 32 * zz + 16 * (seq // 4)
                ghot[hot_top : hot_top + 16, 128 * (seq % 4) : 128 * (seq % 4) + 128] = ah[core, yy, 0, zz].astype(F32)
    hits = [
        (iota((256, 128), 0) + g * 256 == asked[i : i + 1, :]).astype(F32).astype(BF16) for i in range(4)
    ]
    gcold[...] = mm(jnp.concatenate(hits, axis=1), ret[...].reshape(512, 512))


def on_device(
    d_out, weight_in, weight_out, hot_table, cold_table, cold_ids, cold_counts, event_slots, lengths
):
    ids = jnp.pad(cold_ids.reshape(8, 16, 4).transpose(1, 0, 2), ((0, 0), (0, 0), (0, 124)))
    slot = event_slots.reshape(512)
    cold = slot - 512
    owner, part = cold // 4, cold % 4
    code = jnp.where(slot < 512, slot, 512 + owner % 16 * 32 + owner // 16 * 4 + part)
    code_col = jnp.broadcast_to(code[:, None], (512, 128))
    code_row = code.reshape(1, 512)
    valid = jnp.arange(4, dtype=jnp.int32)[None, None, :] < cold_counts.reshape(8, 16).T[:, :, None]
    valid = valid.astype(jnp.int32).reshape(512)
    valid_row = valid.reshape(1, 512)
    valid_col = jnp.broadcast_to(valid[:, None], (512, 128))
    inv = 1.0 / lengths.astype(F32)

    vmem = pl.BlockSpec(memory_space=pltpu.VMEM)
    smem = pl.BlockSpec(memory_space=pltpu.SMEM)
    big = lambda *shape: pltpu.VMEM(shape, BF16)
    wide = lambda *shape: pltpu.VMEM(shape, F32)
    sems = pltpu.SemaphoreType.DMA
    outs = [jax.ShapeDtypeStruct((2, 4, 4, 4, 16, w), BF16) for w in (*AG_WIDTHS, 128)] + [
        jax.ShapeDtypeStruct((4, 8, 16, 512), BF16),
        jax.ShapeDtypeStruct((8, 128), jnp.int32),
    ]
    scratch = [
        pltpu.VMEM((16, 8, 128), jnp.int32),
        pltpu.VMEM((8, 16, 128), jnp.int32),
        big(4, 8, 16, 512),
        big(8, 4, 16, 512),
        big(16, 32, 512),
        big(16, 32, 512),
        big(2, 256, 512),
        big(8, 256, 512),
        big(8, 256, 512),
        big(512, 512),
        big(512, 512),
        sems((4,)),
        wide(512, 2048),
        big(128, 2048),
        big(128, 2048),
        big(128, 2048),
        big(128, 2048),
        big(2048, 128),
        big(2048, 128),
        big(2048, 128),
        big(10, 512, 512),
        big(10, 512, 512),
        wide(128, 2048),
        wide(128, 2048),
        big(128, 2048),
        big(128, 2048),
        big(2048, 128),
        wide(128, 2048),
        wide(2048, 128),
        wide(2048, 128),
        big(512, 2048),
        wide(4, 2, 2048),
        wide(4, 2, 2048),
        big(4, 512, 256),
        big(4, 512, 256),
        big(4, 512, 256),
        big(4, 512, 256),
        big(512, 512),
        big(16, 32, 640),
        big(16, 32, 640),
        big(2, 16, 640),
        big(16, 640),
        big(16, 32, 512),
        big(16, 32, 512),
        big(8, 16, 128),
        big(8, 16, 128),
        big(16, 32, 512),
        big(16, 32, 512),
        big(8, 4, 16, 512),
        sems((5, 2, 16)),
        sems((4, 2, 8)),
        sems((5, 2, 4)),
        sems((4, 3, 2, 4)),
        sems((5, 2, 4)),
    ]
    a0, a1, a2, ah, ret, asked = pl.pallas_call(
        main_kernel,
        out_shape=outs,
        in_specs=[vmem] * 5 + [smem] * 2 + [vmem] * 4 + [pl.BlockSpec(memory_space=pl.ANY)],
        out_specs=[vmem] * 6,
        scratch_shapes=scratch,
        compiler_params=pltpu.CompilerParams(
            collective_id=0, has_side_effects=True, vmem_limit_bytes=60 * 1024 * 1024
        ),
        name="layer",
    )(
        ids, code_col, code_row, valid_row, valid_col, lengths, inv,
        d_out, weight_out, hot_table, cold_table, weight_in,
    )

    def ag_spec(w):
        return pl.BlockSpec((2, 4, 1, 2, 16, w), lambda g: (0, 0, g // 2, lax.rem(g, 2), 0, 0))

    return pl.pallas_call(
        finish_kernel,
        grid=(8,),
        out_shape=[
            jax.ShapeDtypeStruct((512, 2048), F32),
            jax.ShapeDtypeStruct((512, 512), F32),
            jax.ShapeDtypeStruct((512, 512), F32),
            jax.ShapeDtypeStruct((2048, 512), F32),
        ],
        in_specs=[ag_spec(w) for w in (*AG_WIDTHS, 128)]
        + [
            pl.BlockSpec((4, 8, 16, 512), lambda g: (0, 0, 0, 0)),
            pl.BlockSpec((8, 128), lambda g: (0, 0)),
        ],
        out_specs=[
            pl.BlockSpec((64, 2048), lambda g: (g, 0)),
            pl.BlockSpec((512, 512), lambda g: (0, 0)),
            pl.BlockSpec((64, 512), lambda g: (g, 0)),
            pl.BlockSpec((256, 512), lambda g: (g, 0)),
        ],
        compiler_params=pltpu.CompilerParams(vmem_limit_bytes=32 * 1024 * 1024),
        name="finish",
    )(a0, a1, a2, ah, ret, asked)


def solution(mesh):
    placed = (
        P("own", "seq", None),
        P(),
        P(),
        P(),
        P(("seq", "own"), None),
        P(("seq", "own"), None),
        P(("seq", "own")),
        P("own", "seq"),
        P("own"),
    )
    return jax.shard_map(
        on_device,
        mesh=mesh,
        in_specs=placed,
        out_specs=(P(), P(), P(), P(("seq", "own"), None)),
        check_vma=False,
    )
```

time: 505 us -> 163 us (0.32); the launches traced: 498 us -> 162 us
  waiting for transfers between devices: 279 us -> 0 us
  Pallas kernels: 0 us -> 147 us
  matrix products: 76.3 us -> 0 us
  local copies, waits for them, and re-layouts: 60.3 us -> 12.4 us
  other arithmetic: 42.9 us -> 1.91 us
  starting transfers between devices: 25.1 us -> 0 us
  between operations: 14.6 us -> 0.69 us
    pallas_call x0 -> x2, Pallas kernels: none -> 147 us  [the longest x1 141 us: on_device(): pl.pallas_call(main_kernel, out_shape=outs, in_specs=[vmem] * 5 + [smem]...]
    psum x1 -> x0, waiting for transfers between devices: 122 us -> none  [on_device(): summed = lax.psum((grad_w_in, grad_w_out, hot_sum), ('seq', 'own'))]
    reduce_scatter x1 -> x0, waiting for transfers between devices: 77.5 us -> none  [on_device(): lax.psum_scatter(partial_kv, 'seq', scatter_dimension=1, tiled=True)]
    dot_general x11 -> x0, matrix products: 76.3 us -> none  [the longest x1 14.4 us: on_device(): jnp.einsum('uthd,ushd->uhts', grad_heads, value_heads, preferred_element_...]
    all_gather x1 -> x0, waiting for transfers between devices: 42.2 us -> none  [on_device(): keyval_all = lax.all_gather(keyval_local, 'seq', axis=1, tiled=True)]
    all_to_all x3 -> x0, waiting for transfers between devices: 37.4 us -> none  [the longest x1 19.6 us: on_device(): lax.all_to_all(slot_sum, ('seq', 'own'), split_axis=0, concat_axis=0, til...]
    reshape x10 -> x3, local copies, waits for them, and re-layouts: 30.6 us -> 1.63 us  [the longest x2 0.9 us: on_device(): cold_ids.reshape(8, 16, 4).transpose(1, 0, 2)]
    all_to_all x3 -> x0, starting transfers between devices: 25 us -> none  [the longest x1 11.5 us: on_device(): lax.all_to_all(cold_ids, ('seq', 'own'), split_axis=0, concat_axis=0, til...]
  transfers between devices with their start and end apart: 6 -> 0, of which waited for: 6 -> 0; matrix products, arithmetic and copies ran while one was open for 8% -> 0% of each run, Pallas kernels for 0% -> 0%
where the time goes in v1:
time: 163 us; the launch traced here: 162 us
  Pallas kernels  147 us (90%)
  local copies, waits for them, and re-layouts  12.4 us (8%)
  other arithmetic  1.91 us (1%)
    pallas_call x1, Pallas kernels, on_device(): pl.pallas_call(main_kernel, out_shape=outs, in_specs=[vmem] * 5 + [smem]...  141 us
    unnamed x14, local copies, waits for them, and re-layouts  7.61 us
    pallas_call x1, Pallas kernels, on_device(): pl.pallas_call(finish_kernel, grid=(8,), out_shape=[jax.ShapeDtypeStruct(...  5.84 us

profile of v1, /device:TPU:1, one launch (start us, length us, event | category | flops | bytes accessed | tf_op | source)
XLA Modules:
  0.0 162.1 jit_solution(1082824474734693989)
XLA Ops:
  0.6 1.2 convert_divide_fusion.inv_ref
  1.8 0.7 copy.16
  2.5 0.7 copy.17
  3.2 0.6 compare_select_fusion.code_row
  3.8 0.7 reshape.309
  4.6 0.1 copy.15
  4.6 0.8 reshape.306
  5.4 0.1 copy.14
  5.5 0.6 pad.4.ids_ref
  6.2 0.1 fusion
  6.3 0.1 reshape.311
  6.4 0.7 reshape.310.valid_row
  7.1 0.8 broadcast_in_dim.5.valid_col
  7.9 0.8 broadcast_in_dim.4.code_col
  8.7 141.2 %layer.1 = (bf16[2,4,4,4,16,256]{5,4,3,2,1,0:T(8,128)(2,1)}, bf16[2,4,4,4,16,256]{5,4,3,2,1,0:T(8,128)(2,1)}, bf16[2,4,4,4,16,128]{5,4,3,2,1,0:T(8,128)(2,1)}, b...) custom-call(s32[16,8,128]{2,1,0:T(8,128)} %pad.4.ids_ref, ...), custom_call_target="tpu_custom_call" | custom-call | tf_op jit(solution)/shard_map/layer/pallas_call | solution.py:583
  150.0 0.0 copy-start
  150.0 1.2 copy-done
  151.2 0.0 copy-start.1
  151.2 1.2 copy-done.1
  152.4 0.0 copy-start.2
  152.4 1.0 copy-done.2
  153.5 0.0 copy-start.3
  153.5 1.0 copy-done.3
  154.5 0.0 copy-start.4
  154.5 1.0 copy-done.4
  155.6 0.0 copy-start.5
  155.6 0.7 copy-done.5
  156.2 5.8 %finish.1 = (f32[512,2048]{1,0:T(8,128)}, f32[512,512]{1,0:T(8,128)}, f32[512,512]{1,0:T(8,128)}, f32[2048,512]{1,0:T(8,128)}) custom-call(bf16[2,4,4,4,16,256]{5,4,3,2,1,0:T(8,128)(2,1)S(1)} %copy-done, bf16[2,4,4,4,16,256]{5,4,3,2,1,0:T(8,128)(2,1)S(1)} %copy-done.1, bf16[2,4,4,4,16,128]{5,4,3,2,1,0:T(8,128)(2,1)S(1)} %copy-done.2, ...), custom_call_target="tpu_custom_call" | custom-call | tf_op jit(solution)/shard_map/finish/pallas_call | solution.py:601
  (1 shorter events, 0.0 us)
Async XLA Ops:
  150.0 1.2 copy-start
  151.2 1.2 copy-start.1
  152.4 1.0 copy-start.2
  153.5 1.0 copy-start.3
  154.5 1.0 copy-start.4
  155.6 0.7 copy-start.5

commit v2 on v1

v2 whole, which is shorter than its diff:
```python
import functools

import jax
import jax.numpy as jnp
from jax import lax
from jax.experimental import pallas as pl
from jax.experimental.pallas import tpu as pltpu
from jax.sharding import PartitionSpec as P

F32 = jnp.float32
BF16 = jnp.bfloat16
MESH = pl.DeviceIdType.MESH
SCALE = 128 ** (-0.5)
AG_ORDERS = (("z", "x", "y"), ("x", "y", "z"), ("y", "z", "x"))
CHUNKS = 2
CW = 512 // CHUNKS


def mm(a, b):
    return jnp.dot(a, b, preferred_element_type=F32)


def mm_nt(a, b):
    return lax.dot_general(a, b, (((1,), (1,)), ((), ())), preferred_element_type=F32)


def iota(shape, dim):
    return lax.broadcasted_iota(jnp.int32, shape, dim)


def onehot(hit):
    return hit.astype(F32).astype(BF16)


class Exchange:
    def __init__(self, n, me, device, src, dst, send_sem, recv_sem):
        self.n, self.me, self.device, self.src, self.dst = n, me, device, src, dst
        self.send_sem, self.recv_sem = send_sem, recv_sem

    def _out(self, p):
        return pltpu.make_async_remote_copy(
            src_ref=self.src(p),
            dst_ref=self.dst(self.me),
            send_sem=self.send_sem.at[p],
            recv_sem=self.recv_sem.at[self.me],
            device_id=self.device(p),
            device_id_type=MESH,
        )

    def _in(self, p):
        return pltpu.make_async_remote_copy(
            src_ref=self.src(p),
            dst_ref=self.dst(p),
            send_sem=self.send_sem.at[p],
            recv_sem=self.recv_sem.at[p],
            device_id=self.device(p),
            device_id_type=MESH,
        )

    def peer(self, k):
        return lax.rem(self.me + k, self.n)

    def _each(self, f):
        if self.n <= 4:
            for k in range(1, self.n):
                f(self.peer(k))
        else:
            pl.loop(1, self.n)(lambda k: f(self.peer(k)))

    def start(self, pending):
        pending.append(self.wait_send)
        self._each(lambda p: self._out(p).start())

    def start_to(self, p, pending):
        pending.append(lambda: self._out(p).wait_send())
        self._out(p).start()

    def wait_from(self, p):
        self._in(p).wait_recv()

    def wait_recv(self):
        self._each(lambda p: self._in(p).wait_recv())

    def wait_send(self):
        self._each(lambda p: self._out(p).wait_send())


def main_kernel(
    idst_ref, counts_ref, ev_ref, len_ref, dout_ref, wout_ref, hot_ref, table_ref, win_ref,
    ag0, ag1, ag2, ret, asked,
    id_pad, id_loc, id_a, id_b, ev_loc, ev_all, code_col, valid_col,
    got, rows, perm, fetched, e_loc, e_all, c_all,
    wh, wht, wh_sem, slope_pre, u_t, q_t, k_t, v_t, q_n, k_n, v_n,
    w_st, sl_st, att, gg, gat, ga_t, ga_n, gq, gk, gv, g_t, stat,
    sib_s, sib_r, own_p, y_s, y_r, grad, w_send, w_recv, wu_s, wu_r, hu_s, hu_r,
    s_send, q_recv, p_send,
    sem16, sem8, sem4, sem_ag, sem_sib,
):
    s, o = lax.axis_index("seq"), lax.axis_index("own")
    y, c = s // 2, lax.rem(s, 2)
    u, h = s // 4, lax.rem(s, 4)
    x, z = o // 4, lax.rem(o, 4)
    sib = (2 * y + 1 - c, o)
    ags = (ag0, ag1, ag2)
    chunks = range(CHUNKS)
    pending = []

    barrier = pltpu.get_barrier_semaphore()

    @pl.loop(1, 16)
    def _(k):
        pl.semaphore_signal(barrier, inc=1, device_id=(s, lax.rem(o + k, 16)), device_id_type=MESH)

    @pl.loop(1, 8)
    def _(k):
        pl.semaphore_signal(barrier, inc=1, device_id=(lax.rem(s + k, 8), o), device_id_type=MESH)

    def load_w(b):
        return pltpu.make_async_copy(
            win_ref.at[:, pl.ds(pl.multiple_of(b * 512 + h * 128, 128), 128)],
            wh.at[:, pl.ds(b * 128, 128)],
            wh_sem.at[b],
        )

    for b in range(4):
        load_w(b).start()

    def own_x(i, src, dst):
        return Exchange(16, o, lambda p: (s, p), src, dst, sem16.at[i, 0], sem16.at[i, 1])

    def seq_x(i, src, dst):
        return Exchange(8, s, lambda p: (p, o), src, dst, sem8.at[i, 0], sem8.at[i, 1])

    def y_x(i, src, dst):
        return Exchange(4, y, lambda p: (2 * p + c, o), src, dst, sem4.at[i, 0], sem4.at[i, 1])

    def head_x(i, src, dst):
        return Exchange(4, h, lambda p: (4 * u + p, o), src, dst, sem4.at[i, 0], sem4.at[i, 1])

    def to_sib(src, dst, i, j):
        return pltpu.make_async_remote_copy(
            src_ref=src, dst_ref=dst, send_sem=sem_sib.at[i, 0, j], recv_sem=sem_sib.at[i, 1, j],
            device_id=sib, device_id_type=MESH,
        )

    def start_sib(copy):
        pending.append(copy.wait_send)
        copy.start()

    ids_x1 = own_x(0, lambda p: id_loc.at[:, p], lambda p: id_a.at[p])
    ids_x2 = seq_x(0, lambda p: id_a.at[:, p], lambda p: id_b.at[p])
    ev_x = seq_x(1, lambda p: ev_loc.at[p // 4], lambda p: ev_all.at[p])
    hot_x = seq_x(2, lambda p: hu_s.at[p], lambda p: hu_r.at[p])
    rows_x1 = [seq_x(3 + k, lambda p, k=k: got.at[k, :, p], lambda p, k=k: rows.at[k, p]) for k in chunks]
    ret_x2 = [
        seq_x(3 + CHUNKS + k, lambda p, k=k: p_send.at[k, p], lambda p, k=k: ret.at[k, :, p]) for k in chunks
    ]
    w_x = own_x(1, lambda p: w_send.at[p], lambda p: w_recv.at[p])
    rows_x2 = [own_x(2 + k, lambda p, k=k: perm.at[k, p], lambda p, k=k: fetched.at[k, p]) for k in chunks]
    ret_x1 = [
        own_x(2 + CHUNKS + k, lambda p, k=k: s_send.at[k, p], lambda p, k=k: q_recv.at[k, p]) for k in chunks
    ]
    cot_x = y_x(0, lambda p: dout_ref.at[p // 2], lambda p: c_all.at[2 * p + c])
    stat_x = head_x(1, lambda p: stat.at[h], lambda p: stat.at[p])
    emb_x = [
        y_x(2 + k, lambda p, k=k: e_loc.at[k, p // 2], lambda p, k=k: e_all.at[k, 2 * p + c]) for k in chunks
    ]
    grad_x = [y_x(2 + CHUNKS + k, lambda p, k=k: y_s.at[k, p], lambda p, k=k: y_r.at[k, p]) for k in chunks]

    def sib_block(buf, i, yy):
        return to_sib(buf.at[2 * yy + c], buf.at[2 * yy + c], i, yy)

    def sib_block_in(buf, i, yy):
        return to_sib(buf.at[2 * yy + 1 - c], buf.at[2 * yy + 1 - c], i, yy)

    id_pad[...] = jnp.zeros_like(id_pad)
    id_pad[0:4, :] = idst_ref[...]
    id_loc[...] = id_pad[...].T.reshape(8, 16, 128)

    pl.semaphore_wait(barrier, 22)

    ids_x1.start(pending)
    id_a[o] = id_loc[:, o, :]
    for d in (1, 3):
        cot_x.start_to(lax.rem(y + d, 4), pending)
    c_all[s] = dout_ref[u]

    codes = []
    for uu in range(2):
        e = ev_ref[uu : uu + 1, :]
        cold = e - 512
        code = jnp.where(e < 512, e, 512 + ((cold >> 2) & 15) * 32 + (cold >> 6) * 4 + (cold & 3))
        ev_loc[uu] = jnp.broadcast_to(code, (8, 256))
        codes.append(code)
    code_row = jnp.concatenate(codes, axis=1)
    code_col[...] = jnp.broadcast_to(code_row, (128, 512)).T
    counts = counts_ref[...].astype(F32).astype(BF16)
    l = iota((128, 512), 1)
    pick = onehot(iota((128, 512), 0) == ((l >> 2) & 7) * 16 + (l >> 5))
    valid_row = (iota((8, 512), 1) & 3).astype(F32) < mm(jnp.broadcast_to(counts, (8, 128)), pick)
    valid_row = valid_row[0:1]
    l = iota((512, 128), 0)
    pick = onehot(iota((512, 128), 1) == ((l >> 2) & 7) * 16 + (l >> 5))
    valid_col[...] = (
        (l & 3).astype(F32) < mm_nt(pick, jnp.broadcast_to(counts, (128, 128)))
    ).astype(F32)
    for b in range(4):
        load_w(b).wait()
    wht[...] = wh[...].T

    ids_x1.wait_recv()
    ids_x2.start(pending)
    id_b[s] = id_a[:, s, :]
    ids_x2.wait_recv()

    asked_ids = id_b[...].reshape(128, 128)
    for i in range(4):
        hit = onehot(iota((128, 2048), 1) == asked_ids[:, i : i + 1])
        found = mm(hit, table_ref[...]).astype(BF16)
        for k in chunks:
            got[k, i] = found[:, k * CW : (k + 1) * CW].reshape(8, 16, CW)
    for k in chunks:
        rows_x1[k].start(pending)
        rows[k, s] = got[k, :, s]
    ev_x.start(pending)
    ev_all[s] = ev_loc[u]
    asked[...] = asked_ids.T[0:8, :]
    start_sib(sib_block(c_all, 0, y))
    hot_hits = [onehot(code_col[...] == iota((512, 128), 1) + b * 128) for b in range(4)]
    emb = mm(jnp.concatenate(hot_hits, axis=1), hot_ref[...])
    r = iota((512, 512), 0)
    pick = onehot(iota((512, 512), 1) == (r & 31) * 16 + (r >> 5))
    for k in chunks:
        rows_x1[k].wait_recv()
        perm[k] = mm(pick, rows[k].reshape(512, CW)).astype(BF16).reshape(16, 32, CW)
        rows_x2[k].start(pending)
        fetched[k, o] = perm[k, o]
    cot_x.start_to(lax.rem(y + 2, 4), pending)
    for d in (1, 3):
        cot_x.wait_from(lax.rem(y + d, 4))
        start_sib(sib_block(c_all, 0, lax.rem(y + d, 4)))
    cold_hits = [
        onehot(jnp.logical_and(
            code_col[...] == iota((512, 128), 1) + (512 + b * 128), valid_row[:, b * 128 : (b + 1) * 128]
        ))
        for b in range(4)
    ]
    cold_hits = jnp.concatenate(cold_hits, axis=1)
    for k in chunks:
        rows_x2[k].wait_recv()
        part = emb[:, k * CW : (k + 1) * CW] + mm(cold_hits, fetched[k].reshape(512, CW))
        e_loc[k] = part.astype(BF16).reshape(2, 256, CW)
        emb_x[k].start(pending)
        e_all[k, s] = e_loc[k, u]
        start_sib(sib_block(e_all.at[k], 2 + k, y))

    def project(blk):
        cols = pl.ds(pl.multiple_of(blk * 256, 256), 256)
        pre = mm_nt(wht[...], jnp.concatenate([e_all[k, blk] for k in chunks], axis=1))
        sig = 0.5 + 0.5 * jnp.tanh(0.5 * pre)
        act = pre * sig
        slope_pre[:, cols] = sig + act * (1.0 - sig)
        act = act.astype(BF16)
        u_t[:, cols] = act[0:128]
        q_t[:, cols] = act[128:256]
        k_t[:, cols] = act[256:384]
        keep = (blk * 256 + iota((1, 256), 1) < len_ref[u]).astype(F32)
        val = (act[384:512].astype(F32) * keep).astype(BF16)
        v_t[:, cols] = val
        q_n[cols, :] = act[128:256].T
        k_n[cols, :] = act[256:384].T
        v_n[cols, :] = val.T

    cot_x.wait_from(lax.rem(y + 2, 4))
    start_sib(sib_block(c_all, 0, lax.rem(y + 2, 4)))
    project(s)
    for k in chunks:
        for d in (1, 3, 2):
            yy = lax.rem(y + d, 4)
            emb_x[k].wait_from(yy)
            start_sib(sib_block(e_all.at[k], 2 + k, yy))
            if k == CHUNKS - 1:
                project(2 * yy + c)
    for d in (0, 1, 3, 2):
        yy = lax.rem(y + d, 4)
        for k in chunks:
            sib_block_in(e_all.at[k], 2 + k, yy).wait_recv()
        project(2 * yy + 1 - c)

    att[...] = jnp.zeros_like(att)

    def forward(i, j, diag):
        keys = pl.multiple_of(j * 512, 512)
        qs = pl.ds(pl.multiple_of(i * 512, 512), 512)
        at = i * (i + 1) // 2 + j
        for m in range(4):
            half = mm(k_n[pl.ds(keys + m * 128, 128), :], q_t[:, qs]) * (0.5 * SCALE)
            t = jnp.tanh(half)
            a = 1.0 + t
            w = half * a
            slope = a * ((1.0 + 2.0 * half) - w)
            if diag:
                ok = iota((128, 512), 0) + m * 128 <= iota((128, 512), 1)
                w = jnp.where(ok, w, 0.0)
                slope = jnp.where(ok, slope, 0.0)
            w_st[at, m * 128 : (m + 1) * 128, :] = w.astype(BF16)
            sl_st[at, m * 128 : (m + 1) * 128, :] = slope.astype(BF16)
        att[:, qs] += mm(v_t[:, pl.ds(keys, 512)], w_st[at])

    @pl.loop(0, 4)
    def _(i):
        @pl.loop(0, i)
        def _(j):
            forward(i, j, False)

        forward(i, i, True)

    for d in range(4):
        sib_block_in(c_all, 0, lax.rem(y + d, 4)).wait_recv()
    live = (iota((1, 2048), 1) < len_ref[u]).astype(F32)
    wo = wout_ref[pl.ds(pl.multiple_of(h * 128, 128), 128), :]
    gg[...] = mm_nt(wo, c_all[...].reshape(2048, 512)) * live
    inv = 1.0 / jnp.full((1, 2048), len_ref[u], jnp.int32).astype(F32)
    mine = att[...] * inv
    m1 = jnp.sum(mine, axis=0, keepdims=True) * (1.0 / 128)
    dev = mine - m1
    gn = gg[...] * u_t[...].astype(F32)
    stat[h, 0:1, :] = m1
    stat[h, 1:2, :] = jnp.sum(dev * dev, axis=0, keepdims=True)
    stat[h, 2:3, :] = jnp.sum(gn, axis=0, keepdims=True)
    stat[h, 3:4, :] = jnp.sum(gn * dev, axis=0, keepdims=True)
    stat_x.start(pending)
    stat_x.wait_recv()
    both = stat[...]
    mean = jnp.sum(both[:, 0, :], axis=0, keepdims=True) * 0.25
    off = both[:, 0, :] - mean
    var = (jnp.sum(both[:, 1, :], axis=0, keepdims=True) + 128.0 * jnp.sum(off * off, axis=0, keepdims=True)) * (
        1.0 / 512
    )
    rstd = lax.rsqrt(var + 1e-05)
    mean1 = jnp.sum(both[:, 2, :], axis=0, keepdims=True) * (1.0 / 512)
    mean2 = jnp.sum(both[:, 3, :] + off * both[:, 2, :], axis=0, keepdims=True) * (rstd * (1.0 / 512))
    normed = (att[...] * inv - mean) * rstd
    att[...] = normed
    gn = gg[...] * u_t[...].astype(F32)
    ga_t[...] = ((gn - mean1 - normed * mean2) * (rstd * inv)).astype(BF16)
    for b in range(8):
        ga_n[b * 256 : (b + 1) * 256, :] = ga_t[:, b * 256 : (b + 1) * 256].T

    gq[...] = jnp.zeros_like(gq)
    gk[...] = jnp.zeros_like(gk)
    gv[...] = jnp.zeros_like(gv)

    def backward(i, j):
        keys = pl.multiple_of(j * 512, 512)
        qs = pl.ds(pl.multiple_of(i * 512, 512), 512)
        at = i * (i + 1) // 2 + j
        for m in range(4):
            gw = mm(v_n[pl.ds(keys + m * 128, 128), :], ga_t[:, qs])
            ds = gw * sl_st[at, m * 128 : (m + 1) * 128, :].astype(F32)
            sl_st[at, m * 128 : (m + 1) * 128, :] = ds.astype(BF16)
        gk[pl.ds(keys, 512), :] += mm(sl_st[at], q_n[qs, :])
        gv[pl.ds(keys, 512), :] += mm(w_st[at], ga_n[qs, :])
        gq[:, qs] += mm(k_t[:, pl.ds(keys, 512)], sl_st[at])

    @pl.loop(0, 4)
    def _(i):
        @pl.loop(0, i + 1)
        def _(j):
            backward(i, j)

    keep = (iota((1, 2048), 1) < len_ref[u]).astype(F32)
    g_t[0:128, :] = (gg[...] * att[...] * slope_pre[0:128, :]).astype(BF16)
    g_t[128:256, :] = (gq[...] * (0.5 * SCALE) * slope_pre[128:256, :]).astype(BF16)
    for b in range(8):
        cols = slice(b * 256, (b + 1) * 256)
        g_t[256:384, cols] = (gk[cols, :].T * (0.5 * SCALE) * slope_pre[256:384, cols]).astype(BF16)
        g_t[384:512, cols] = (gv[cols, :].T * keep[:, cols] * slope_pre[384:512, cols]).astype(BF16)

    def partial(k, blk):
        return mm(wh[k * CW : (k + 1) * CW, :], g_t[:, pl.ds(pl.multiple_of(blk * 256, 256), 256)])

    def sib_grad(k, yy):
        return to_sib(sib_s.at[k, yy], sib_r.at[k, yy], 2 + CHUNKS + k, yy)

    for k in chunks:
        for d in (2, 1, 3, 0):
            yy = lax.rem(y + d, 4)
            sib_s[k, yy] = partial(k, 2 * yy + 1 - c).astype(BF16)
            start_sib(sib_grad(k, yy))
        for d in (2, 1, 3, 0):
            yy = lax.rem(y + d, 4)
            total = partial(k, 2 * yy + c)
            own_p[k, yy] = total.astype(BF16)
            sib_grad(k, yy).wait_recv()
            total = (total + sib_r[k, yy].astype(F32)).astype(BF16)
            if d == 0:
                y_r[k, yy] = total
            else:
                y_s[k, yy] = total
                grad_x[k].start_to(yy, pending)

    gat[...] = (att[...] * u_t[...].astype(F32) * live).astype(BF16)
    gw_out = mm(gat[...], c_all[...].reshape(2048, 512))
    for b in range(4):
        w_send[4 * b : 4 * b + 4, :, 512:640] = gw_out[:, b * 128 : (b + 1) * 128].astype(BF16).reshape(4, 32, 128)
    for k in chunks:
        gw_in = mm(g_t[...], e_all[k].reshape(2048, CW))
        n = CW // 32
        w_send[k * n : (k + 1) * n, :, 0:512] = gw_in.T.astype(BF16).reshape(n, 32, 512)
    ev_x.wait_recv()
    for k in chunks:
        sums = jnp.zeros((512, CW), F32)
        for yy in range(4):
            for same in range(2):
                blk = 2 * yy + (c if same else 1 - c)
                hit = onehot(iota((512, 256), 0) == ev_all[blk, 0:1, :])
                sums += mm_nt(hit, (own_p if same else sib_s)[k, yy])
        for b in range(2):
            blk = 2 * h + b
            hit = jnp.logical_and(
                iota((512, 256), 0) == ev_all[blk, 0:1, :], blk * 256 + iota((1, 256), 1) < len_ref[u]
            )
            sums += mm(onehot(hit), c_all[blk, :, k * CW : (k + 1) * CW])
        w_send[:, :, 640 + k * CW : 640 + (k + 1) * CW] = sums.astype(BF16).reshape(16, 32, CW)
    w_x.start(pending)
    w_recv[o] = w_send[o]

    cots = []
    for uu in range(2):
        here = (s * 256 + iota((256, 1), 0) < len_ref[uu]).astype(F32)
        cots.append((dout_ref[uu].astype(F32) * here).astype(BF16))
    cot = jnp.concatenate(cots, axis=0)
    hits = []
    for uu in range(2):
        hit = iota((512, 256), 0) + 512 == ev_loc[uu, 0:1, :]
        hits.append(onehot(jnp.logical_and(hit, jnp.concatenate([valid_col[...]] * 2, axis=1) > 0)))
    hits = jnp.concatenate(hits, axis=1)
    for k in chunks:
        grad_x[k].wait_recv()
        for uu in range(2):
            grad[:, uu * 256 : (uu + 1) * 256] = (
                y_r[k, 2 * uu].astype(F32) + y_r[k, 2 * uu + 1].astype(F32)
            ).astype(BF16)
        sums = mm_nt(hits, grad[...]) + mm(hits, cot[:, k * CW : (k + 1) * CW])
        s_send[k] = sums.astype(BF16).reshape(16, 32, CW)
        ret_x1[k].start(pending)
        q_recv[k, o] = s_send[k, o]

    w_x.wait_recv()
    total = jnp.sum(w_recv[...].astype(F32), axis=0)
    wu_s[...] = total[:, 0:640].astype(BF16).reshape(2, 16, 640)
    for i in range(8):
        left = 640 + 128 * (i % 4)
        hu_s[i] = total[16 * (i // 4) : 16 * (i // 4) + 16, left : left + 128].astype(BF16)
    wu = pltpu.make_async_remote_copy(
        src_ref=wu_s.at[1 - u],
        dst_ref=wu_r,
        send_sem=sem_sib.at[1, 0, 0],
        recv_sem=sem_sib.at[1, 1, 0],
        device_id=(lax.rem(s + 4, 8), o),
        device_id_type=MESH,
    )
    start_sib(wu)
    hot_x.start(pending)
    hu_r[s] = hu_s[s]

    r = iota((512, 512), 0)
    pick = onehot(iota((512, 512), 1) == (r & 15) * 32 + (r >> 4))
    for k in chunks:
        ret_x1[k].wait_recv()
        p_send[k] = mm(pick, q_recv[k].reshape(512, CW)).astype(BF16).reshape(8, 4, 16, CW)
        ret_x2[k].start(pending)
        ret[k, :, s] = p_send[k, s]

    place = {"y": y, "x": x, "z": z}
    device = {
        "y": lambda p: (2 * p + c, o),
        "x": lambda p: (s, 4 * p + z),
        "z": lambda p: (s, 4 * x + p),
    }

    def slab(i, core, known):
        at = dict(place)
        at.update(known)
        return ags[i].at[core, at["y"], at["x"], at["z"]]

    def gather_x(i, stage):
        order = AG_ORDERS[i]
        axis = order[stage]
        whole = {a: slice(None) for a in order[:stage]}
        block = lambda p: slab(i, c, {**whole, axis: p})
        return Exchange(
            4, place[axis], device[axis], lambda p: block(place[axis]), block,
            sem_ag.at[i, stage, 0], sem_ag.at[i, stage, 1],
        )

    def last_slab(i, core, p):
        order = AG_ORDERS[i]
        blk = slab(i, core, {order[0]: slice(None), order[1]: slice(None), order[2]: p})
        return to_sib(blk, blk, 2 + 2 * CHUNKS + i, p)

    gathers = [[gather_x(i, stage) for stage in range(3)] for i in range(3)]
    wu.wait_recv()
    pick_u = u.astype(F32)
    mine = total[0:16, 0:640] * (1.0 - pick_u) + total[16:32, 0:640] * pick_u + wu_r[...].astype(F32)
    mine = mine.astype(BF16)
    ag0[c, y, x, z] = mine[:, 0:256]
    ag1[c, y, x, z] = mine[:, 256:512]
    for i in range(2):
        gathers[i][0].start(pending)
    hot_x.wait_recv()
    ag2[c, y, x, z] = jnp.concatenate(
        [mine[:, 512:640], jnp.sum(hu_r[...].astype(F32), axis=0).astype(BF16)], axis=1
    )
    gathers[2][0].start(pending)
    for stage in range(2):
        for i in range(3):
            gathers[i][stage].wait_recv()
            gathers[i][stage + 1].start(pending)
    for i in range(3):
        start_sib(last_slab(i, c, place[AG_ORDERS[i][2]]))
    for d in (1, 3, 2):
        for i in range(3):
            p = lax.rem(place[AG_ORDERS[i][2]] + d, 4)
            gathers[i][2].wait_from(p)
            start_sib(last_slab(i, c, p))
    for k in chunks:
        ret_x2[k].wait_recv()
    for i in range(3):
        for p in range(4):
            last_slab(i, 1 - c, p).wait_recv()

    for wait in pending:
        wait()


def finish_kernel(a0, a1, a2, ret, asked, gin, gout, ghot, gcold):
    g = pl.program_id(0)
    for yy in range(4):
        for core in range(2):
            user, head = yy // 2, (yy % 2) * 2 + core
            seq = 2 * yy + core
            for zz in range(2):
                top = 32 * zz + 16 * user
                b0 = a0[core, yy, 0, zz].astype(F32)
                b1 = a1[core, yy, 0, zz].astype(F32)
                b2 = a2[core, yy, 0, zz].astype(F32)
                for b in range(4):
                    part = (b0, b1)[b // 2][:, (b % 2) * 128 : (b % 2) * 128 + 128]
                    gin[top : top + 16, b * 512 + head * 128 : b * 512 + head * 128 + 128] = part
                low = pl.multiple_of(head * 128 + 32 * (2 * lax.rem(g, 2) + zz) + 16 * user, 16)
                gout[pl.ds(low, 16), pl.ds(pl.multiple_of(g // 2 * 128, 128), 128)] = b2[:, 0:128]
                hot_top = 32 * zz + 16 * (seq // 4)
                ghot[hot_top : hot_top + 16, 128 * (seq % 4) : 128 * (seq % 4) + 128] = b2[:, 128:256]
    hits = jnp.concatenate([onehot(iota((256, 128), 0) + g * 256 == asked[i : i + 1, :]) for i in range(4)], axis=1)
    for k in range(CHUNKS):
        gcold[:, k * CW : (k + 1) * CW] = mm(hits, ret[k].reshape(512, CW))


def on_device(
    d_out, weight_in, weight_out, hot_table, cold_table, cold_ids, cold_counts, event_slots, lengths
):
    vmem = pl.BlockSpec(memory_space=pltpu.VMEM)
    smem = pl.BlockSpec(memory_space=pltpu.SMEM)
    big = lambda *shape: pltpu.VMEM(shape, BF16)
    wide = lambda *shape: pltpu.VMEM(shape, F32)
    sems = pltpu.SemaphoreType.DMA
    outs = [jax.ShapeDtypeStruct((2, 4, 4, 4, 16, 256), BF16)] * 3 + [
        jax.ShapeDtypeStruct((CHUNKS, 4, 8, 16, CW), BF16),
        jax.ShapeDtypeStruct((8, 128), jnp.int32),
    ]
    ints = lambda *shape: pltpu.VMEM(shape, jnp.int32)
    scratch = [
        ints(128, 128),
        ints(8, 16, 128),
        ints(16, 8, 128),
        ints(8, 16, 128),
        ints(2, 8, 256),
        ints(8, 8, 256),
        ints(512, 128),
        wide(512, 128),
        big(CHUNKS, 4, 8, 16, CW),
        big(CHUNKS, 8, 4, 16, CW),
        big(CHUNKS, 16, 32, CW),
        big(CHUNKS, 16, 32, CW),
        big(CHUNKS, 2, 256, CW),
        big(CHUNKS, 8, 256, CW),
        big(8, 256, 512),
        big(512, 512),
        big(512, 512),
        sems((4,)),
        wide(512, 2048),
        big(128, 2048),
        big(128, 2048),
        big(128, 2048),
        big(128, 2048),
        big(2048, 128),
        big(2048, 128),
        big(2048, 128),
        big(10, 512, 512),
        big(10, 512, 512),
        wide(128, 2048),
        wide(128, 2048),
        big(128, 2048),
        big(128, 2048),
        big(2048, 128),
        wide(128, 2048),
        wide(2048, 128),
        wide(2048, 128),
        big(512, 2048),
        wide(4, 4, 2048),
        big(CHUNKS, 4, CW, 256),
        big(CHUNKS, 4, CW, 256),
        big(CHUNKS, 4, CW, 256),
        big(CHUNKS, 4, CW, 256),
        big(CHUNKS, 4, CW, 256),
        big(CW, 512),
        big(16, 32, 1152),
        big(16, 32, 1152),
        big(2, 16, 640),
        big(16, 640),
        big(8, 16, 128),
        big(8, 16, 128),
        big(CHUNKS, 16, 32, CW),
        big(CHUNKS, 16, 32, CW),
        big(CHUNKS, 8, 4, 16, CW),
        sems((2 + 2 * CHUNKS, 2, 16)),
        sems((3 + 2 * CHUNKS, 2, 8)),
        sems((2 + 2 * CHUNKS, 2, 4)),
        sems((3, 3, 2, 4)),
        sems((5 + 2 * CHUNKS, 2, 4)),
    ]
    a0, a1, a2, ret, asked = pl.pallas_call(
        main_kernel,
        out_shape=outs,
        in_specs=[vmem] * 3 + [smem] + [vmem] * 4 + [pl.BlockSpec(memory_space=pl.ANY)],
        out_specs=[vmem] * 5,
        scratch_shapes=scratch,
        compiler_params=pltpu.CompilerParams(
            collective_id=0, has_side_effects=True, vmem_limit_bytes=60 * 1024 * 1024
        ),
        name="layer",
    )(
        cold_ids.T, cold_counts.reshape(1, 128), event_slots, lengths,
        d_out, weight_out, hot_table, cold_table, weight_in,
    )

    part = pl.BlockSpec((2, 4, 1, 2, 16, 256), lambda g: (0, 0, g // 2, lax.rem(g, 2), 0, 0))
    return pl.pallas_call(
        finish_kernel,
        grid=(8,),
        out_shape=[
            jax.ShapeDtypeStruct((512, 2048), F32),
            jax.ShapeDtypeStruct((512, 512), F32),
            jax.ShapeDtypeStruct((512, 512), F32),
            jax.ShapeDtypeStruct((2048, 512), F32),
        ],
        in_specs=[part] * 3
        + [
            pl.BlockSpec((CHUNKS, 4, 8, 16, CW), lambda g: (0, 0, 0, 0, 0)),
            pl.BlockSpec((8, 128), lambda g: (0, 0)),
        ],
        out_specs=[
            pl.BlockSpec((64, 2048), lambda g: (g, 0)),
            pl.BlockSpec((512, 512), lambda g: (0, 0)),
            pl.BlockSpec((64, 512), lambda g: (g, 0)),
            pl.BlockSpec((256, 512), lambda g: (g, 0)),
        ],
        compiler_params=pltpu.CompilerParams(vmem_limit_bytes=60 * 1024 * 1024),
        name="finish",
    )(a0, a1, a2, ret, asked)


def solution(mesh):
    placed = (
        P("own", "seq", None),
        P(),
        P(),
        P(),
        P(("seq", "own"), None),
        P(("seq", "own"), None),
        P(("seq", "own")),
        P("own", "seq"),
        P("own"),
    )
    return jax.shard_map(
        on_device,
        mesh=mesh,
        in_specs=placed,
        out_specs=(P(), P(), P(), P(("seq", "own"), None)),
        check_vma=False,
    )
```

time: 163 us -> 145 us (0.89)
  local copies, waits for them, and re-layouts: 12.4 us -> 0 us
  Pallas kernels: 147 us -> 145 us
  other arithmetic: 1.91 us -> 0 us
    unnamed x14 -> x0, local copies, waits for them, and re-layouts: 7.61 us -> none
    pallas_call x1, Pallas kernels: 141 us -> 136 us  [on_device(): pl.pallas_call(main_kernel, out_shape=outs, in_specs=[vmem] * 3 + [smem]...]
    pallas_call x1, Pallas kernels: 5.84 us -> 8.78 us  [on_device(): pl.pallas_call(finish_kernel, grid=(8,), out_shape=[jax.ShapeDtypeStruct(...]
    broadcast_in_dim x2 -> x0, local copies, waits for them, and re-layouts: 1.67 us -> none  [the longest x1 0.84 us: on_device(): valid_col = jnp.broadcast_to(valid[:, None], (512, 128))]
where the time goes in v2:
time: 145 us
  Pallas kernels  145 us (100%)
    pallas_call x1, Pallas kernels, on_device(): pl.pallas_call(main_kernel, out_shape=outs, in_specs=[vmem] * 3 + [smem]...  136 us
    pallas_call x1, Pallas kernels, on_device(): pl.pallas_call(finish_kernel, grid=(8,), out_shape=[jax.ShapeDtypeStruct(...  8.78 us

profile of v2, /device:TPU:1, one launch (start us, length us, event | category | flops | bytes accessed | tf_op | source)
XLA Modules:
  0.0 145.2 jit_solution(16309176876498827979)
XLA Ops:
  0.6 135.8 %layer.1 = (bf16[2,4,4,4,16,256]{5,4,3,2,1,0:T(8,128)(2,1)}, bf16[2,4,4,4,16,256]{5,4,3,2,1,0:T(8,128)(2,1)}, bf16[2,4,4,4,16,256]{5,4,3,2,1,0:T(8,128)(2,1)}, b...) custom-call(s32[4,128]{1,0:T(4,128)} %bitcast.2, s32[1,128]{1,0:T(1,128)} %bitcast.3, s32[2,256]{1,0:T(2,128)} %ev_ref.1, ...), custom_call_target="tpu_custom_call" | custom-call | tf_op jit(solution)/shard_map/layer/pallas_call | solution.py:634
  136.4 8.8 %finish.1 = (f32[512,2048]{1,0:T(8,128)}, f32[512,512]{1,0:T(8,128)}, f32[512,512]{1,0:T(8,128)}, f32[2048,512]{1,0:T(8,128)}) custom-call(bf16[2,4,4,4,16,256]{5,4,3,2,1,0:T(8,128)(2,1)} %get-tuple-element.9.a0, bf16[2,4,4,4,16,256]{5,4,3,2,1,0:T(8,128)(2,1)} %get-tuple-element.10.a1, bf16[2,4,4,4,16,256]{5,4,3,2,1,0:T(8,128)(2,1)} %get-tuple-element.11.a2, ...), custom_call_target="tpu_custom_call" | custom-call | tf_op jit(solution)/shard_map/finish/pallas_call | solution.py:650

commit v3 on v2

--- a/solution.py
+++ b/solution.py
@@ -12,8 +12,11 @@
 MESH = pl.DeviceIdType.MESH
 SCALE = 128 ** (-0.5)
 AG_ORDERS = (("z", "x", "y"), ("x", "y", "z"), ("y", "z", "x"))
+HEAD = 2
+HW = 512 // HEAD
 CHUNKS = 2
 CW = 512 // CHUNKS
+HALF = 256 // CHUNKS
 
 
 def mm(a, b):
@@ -61,7 +64,7 @@
         return lax.rem(self.me + k, self.n)
 
     def _each(self, f):
-        if self.n <= 4:
+        if self.n <= 16:
             for k in range(1, self.n):
                 f(self.peer(k))
         else:
@@ -86,14 +89,14 @@
 
 
 def main_kernel(
-    idst_ref, counts_ref, ev_ref, len_ref, dout_ref, wout_ref, hot_ref, table_ref, win_ref,
+    idst_ref, counts_ref, ev_ref, len_ref, dout_any, wout_any, hot_any, table_any, win_ref,
     ag0, ag1, ag2, ret, asked,
     id_pad, id_loc, id_a, id_b, ev_loc, ev_all, code_col, valid_col,
     got, rows, perm, fetched, e_loc, e_all, c_all,
     wh, wht, wh_sem, slope_pre, u_t, q_t, k_t, v_t, q_n, k_n, v_n,
     w_st, sl_st, att, gg, gat, ga_t, ga_n, gq, gk, gv, g_t, stat,
-    sib_s, sib_r, own_p, y_s, y_r, grad, w_send, w_recv, wu_s, wu_r, hu_s, hu_r,
-    s_send, q_recv, p_send,
+    sib_s, sib_r, tot, g_r, grad, w1_send, w1_recv, w2_send, w2_recv, wu_s, wu_r, hu_s, hu_r,
+    s_send, q_recv, p_send, dout_ref, wout_ref, hot_ref, table_ref, load_sem,
     sem16, sem8, sem4, sem_ag, sem_sib,
 ):
     s, o = lax.axis_index("seq"), lax.axis_index("own")
@@ -103,6 +106,7 @@
     sib = (2 * y + 1 - c, o)
     ags = (ag0, ag1, ag2)
     chunks = range(CHUNKS)
+    heads = range(HEAD)
     pending = []
 
     barrier = pltpu.get_barrier_semaphore()
@@ -122,6 +126,14 @@
             wh_sem.at[b],
         )
 
+    loads = [
+        pltpu.make_async_copy(a, b, load_sem.at[i])
+        for i, (a, b) in enumerate(
+            ((table_any, table_ref), (dout_any, dout_ref), (hot_any, hot_ref), (wout_any, wout_ref))
+        )
+    ]
+    for copy in loads:
+        copy.start()
     for b in range(4):
         load_w(b).start()
 
@@ -150,22 +162,29 @@
     ids_x1 = own_x(0, lambda p: id_loc.at[:, p], lambda p: id_a.at[p])
     ids_x2 = seq_x(0, lambda p: id_a.at[:, p], lambda p: id_b.at[p])
     ev_x = seq_x(1, lambda p: ev_loc.at[p // 4], lambda p: ev_all.at[p])
-    hot_x = seq_x(2, lambda p: hu_s.at[p], lambda p: hu_r.at[p])
-    rows_x1 = [seq_x(3 + k, lambda p, k=k: got.at[k, :, p], lambda p, k=k: rows.at[k, p]) for k in chunks]
+    rows_x1 = [seq_x(2 + k, lambda p, k=k: got.at[k, :, p], lambda p, k=k: rows.at[k, p]) for k in heads]
     ret_x2 = [
-        seq_x(3 + CHUNKS + k, lambda p, k=k: p_send.at[k, p], lambda p, k=k: ret.at[k, :, p]) for k in chunks
+        seq_x(2 + HEAD + k, lambda p, k=k: p_send.at[k, p], lambda p, k=k: ret.at[k, :, p]) for k in chunks
     ]
-    w_x = own_x(1, lambda p: w_send.at[p], lambda p: w_recv.at[p])
-    rows_x2 = [own_x(2 + k, lambda p, k=k: perm.at[k, p], lambda p, k=k: fetched.at[k, p]) for k in chunks]
+    w1_x = own_x(1, lambda p: w1_send.at[p], lambda p: w1_recv.at[p])
+    w2_x = own_x(2, lambda p: w2_send.at[p], lambda p: w2_recv.at[p])
+    rows_x2 = [own_x(3 + k, lambda p, k=k: perm.at[k, p], lambda p, k=k: fetched.at[k, p]) for k in heads]
     ret_x1 = [
-        own_x(2 + CHUNKS + k, lambda p, k=k: s_send.at[k, p], lambda p, k=k: q_recv.at[k, p]) for k in chunks
+        own_x(3 + HEAD + k, lambda p, k=k: s_send.at[k, p], lambda p, k=k: q_recv.at[k, p]) for k in chunks
     ]
     cot_x = y_x(0, lambda p: dout_ref.at[p // 2], lambda p: c_all.at[2 * p + c])
     stat_x = head_x(1, lambda p: stat.at[h], lambda p: stat.at[p])
     emb_x = [
-        y_x(2 + k, lambda p, k=k: e_loc.at[k, p // 2], lambda p, k=k: e_all.at[k, 2 * p + c]) for k in chunks
+        y_x(2 + k, lambda p, k=k: e_loc.at[k, p // 2], lambda p, k=k: e_all.at[k, 2 * p + c]) for k in heads
     ]
-    grad_x = [y_x(2 + CHUNKS + k, lambda p, k=k: y_s.at[k, p], lambda p, k=k: y_r.at[k, p]) for k in chunks]
+    hot_x = y_x(2 + HEAD, lambda p: hu_s.at[p], lambda p: hu_r.at[p])
+
+    def positions(k, p):
+        return tot.at[k, :, pl.ds(pl.multiple_of(p * 256, 256), 256)]
+
+    grad_x = [
+        seq_x(2 + HEAD + CHUNKS + k, lambda p, k=k: positions(k, p), lambda p, k=k: g_r.at[k, p]) for k in chunks
+    ]
 
     def sib_block(buf, i, yy):
         return to_sib(buf.at[2 * yy + c], buf.at[2 * yy + c], i, yy)
@@ -181,9 +200,6 @@
 
     ids_x1.start(pending)
     id_a[o] = id_loc[:, o, :]
-    for d in (1, 3):
-        cot_x.start_to(lax.rem(y + d, 4), pending)
-    c_all[s] = dout_ref[u]
 
     codes = []
     for uu in range(2):
@@ -207,6 +223,9 @@
     for b in range(4):
         load_w(b).wait()
     wht[...] = wh[...].T
+    for copy in loads:
+        copy.wait()
+    c_all[s] = dout_ref[u]
 
     ids_x1.wait_recv()
     ids_x2.start(pending)
@@ -217,9 +236,9 @@
     for i in range(4):
         hit = onehot(iota((128, 2048), 1) == asked_ids[:, i : i + 1])
         found = mm(hit, table_ref[...]).astype(BF16)
-        for k in chunks:
-            got[k, i] = found[:, k * CW : (k + 1) * CW].reshape(8, 16, CW)
-    for k in chunks:
+        for k in heads:
+            got[k, i] = found[:, k * HW : (k + 1) * HW].reshape(8, 16, HW)
+    for k in heads:
         rows_x1[k].start(pending)
         rows[k, s] = got[k, :, s]
     ev_x.start(pending)
@@ -230,15 +249,13 @@
     emb = mm(jnp.concatenate(hot_hits, axis=1), hot_ref[...])
     r = iota((512, 512), 0)
     pick = onehot(iota((512, 512), 1) == (r & 31) * 16 + (r >> 5))
-    for k in chunks:
+    for k in heads:
         rows_x1[k].wait_recv()
-        perm[k] = mm(pick, rows[k].reshape(512, CW)).astype(BF16).reshape(16, 32, CW)
+        perm[k] = mm(pick, rows[k].reshape(512, HW)).astype(BF16).reshape(16, 32, HW)
         rows_x2[k].start(pending)
         fetched[k, o] = perm[k, o]
-    cot_x.start_to(lax.rem(y + 2, 4), pending)
     for d in (1, 3):
-        cot_x.wait_from(lax.rem(y + d, 4))
-        start_sib(sib_block(c_all, 0, lax.rem(y + d, 4)))
+        cot_x.start_to(lax.rem(y + d, 4), pending)
     cold_hits = [
         onehot(jnp.logical_and(
             code_col[...] == iota((512, 128), 1) + (512 + b * 128), valid_row[:, b * 128 : (b + 1) * 128]
@@ -246,17 +263,17 @@
         for b in range(4)
     ]
     cold_hits = jnp.concatenate(cold_hits, axis=1)
-    for k in chunks:
+    for k in heads:
         rows_x2[k].wait_recv()
-        part = emb[:, k * CW : (k + 1) * CW] + mm(cold_hits, fetched[k].reshape(512, CW))
-        e_loc[k] = part.astype(BF16).reshape(2, 256, CW)
+        part = emb[:, k * HW : (k + 1) * HW] + mm(cold_hits, fetched[k].reshape(512, HW))
+        e_loc[k] = part.astype(BF16).reshape(2, 256, HW)
         emb_x[k].start(pending)
         e_all[k, s] = e_loc[k, u]
         start_sib(sib_block(e_all.at[k], 2 + k, y))
 
     def project(blk):
         cols = pl.ds(pl.multiple_of(blk * 256, 256), 256)
-        pre = mm_nt(wht[...], jnp.concatenate([e_all[k, blk] for k in chunks], axis=1))
+        pre = mm_nt(wht[...], jnp.concatenate([e_all[k, blk] for k in heads], axis=1))
         sig = 0.5 + 0.5 * jnp.tanh(0.5 * pre)
         act = pre * sig
         slope_pre[:, cols] = sig + act * (1.0 - sig)
@@ -271,19 +288,21 @@
         k_n[cols, :] = act[256:384].T
         v_n[cols, :] = val.T
 
-    cot_x.wait_from(lax.rem(y + 2, 4))
-    start_sib(sib_block(c_all, 0, lax.rem(y + 2, 4)))
+    for d in (1, 3):
+        cot_x.wait_from(lax.rem(y + d, 4))
+        start_sib(sib_block(c_all, 0, lax.rem(y + d, 4)))
     project(s)
-    for k in chunks:
+    for k in heads:
         for d in (1, 3, 2):
             yy = lax.rem(y + d, 4)
             emb_x[k].wait_from(yy)
             start_sib(sib_block(e_all.at[k], 2 + k, yy))
-            if k == CHUNKS - 1:
+            if k == HEAD - 1:
                 project(2 * yy + c)
+    cot_x.start_to(lax.rem(y + 2, 4), pending)
     for d in (0, 1, 3, 2):
         yy = lax.rem(y + d, 4)
-        for k in chunks:
+        for k in heads:
             sib_block_in(e_all.at[k], 2 + k, yy).wait_recv()
         project(2 * yy + 1 - c)
 
@@ -315,6 +334,8 @@
 
         forward(i, i, True)
 
+    cot_x.wait_from(lax.rem(y + 2, 4))
+    start_sib(sib_block(c_all, 0, lax.rem(y + 2, 4)))
     for d in range(4):
         sib_block_in(c_all, 0, lax.rem(y + d, 4)).wait_recv()
     live = (iota((1, 2048), 1) < len_ref[u]).astype(F32)
@@ -347,6 +368,21 @@
     for b in range(8):
         ga_n[b * 256 : (b + 1) * 256, :] = ga_t[:, b * 256 : (b + 1) * 256].T
 
+    def to_rows(rows_by_cols):
+        n = rows_by_cols.shape[1]
+        return rows_by_cols.astype(BF16).reshape(-1, 32, n)
+
+    gat[...] = (att[...] * u_t[...].astype(F32) * live).astype(BF16)
+    gw_out = mm(gat[...], c_all[...].reshape(2048, 512))
+    for b in range(4):
+        w1_send[4 * b : 4 * b + 4, :, 0:128] = to_rows(gw_out[:, b * 128 : (b + 1) * 128])
+    g_t[0:128, :] = (gg[...] * att[...] * slope_pre[0:128, :]).astype(BF16)
+    n = HW // 32
+    for k in heads:
+        w1_send[k * n : (k + 1) * n, :, 128:256] = to_rows(mm(g_t[0:128, :], e_all[k].reshape(2048, HW)).T)
+    w1_x.start(pending)
+    w1_recv[o] = w1_send[o]
+
     gq[...] = jnp.zeros_like(gq)
     gk[...] = jnp.zeros_like(gk)
     gv[...] = jnp.zeros_like(gv)
@@ -370,61 +406,44 @@
             backward(i, j)
 
     keep = (iota((1, 2048), 1) < len_ref[u]).astype(F32)
-    g_t[0:128, :] = (gg[...] * att[...] * slope_pre[0:128, :]).astype(BF16)
     g_t[128:256, :] = (gq[...] * (0.5 * SCALE) * slope_pre[128:256, :]).astype(BF16)
     for b in range(8):
         cols = slice(b * 256, (b + 1) * 256)
         g_t[256:384, cols] = (gk[cols, :].T * (0.5 * SCALE) * slope_pre[256:384, cols]).astype(BF16)
         g_t[384:512, cols] = (gv[cols, :].T * keep[:, cols] * slope_pre[384:512, cols]).astype(BF16)
 
-    def partial(k, blk):
-        return mm(wh[k * CW : (k + 1) * CW, :], g_t[:, pl.ds(pl.multiple_of(blk * 256, 256), 256)])
-
-    def sib_grad(k, yy):
-        return to_sib(sib_s.at[k, yy], sib_r.at[k, yy], 2 + CHUNKS + k, yy)
+    def partial(k, half):
+        return mm(wh[pl.ds(pl.multiple_of(half * 256 + k * HALF, HALF), HALF), :], g_t[...])
+
+    def sib_grad(k):
+        return to_sib(sib_s.at[k], sib_r.at[k], 2 + HEAD, k)
 
     for k in chunks:
-        for d in (2, 1, 3, 0):
-            yy = lax.rem(y + d, 4)
-            sib_s[k, yy] = partial(k, 2 * yy + 1 - c).astype(BF16)
-            start_sib(sib_grad(k, yy))
-        for d in (2, 1, 3, 0):
-            yy = lax.rem(y + d, 4)
-            total = partial(k, 2 * yy + c)
-            own_p[k, yy] = total.astype(BF16)
-            sib_grad(k, yy).wait_recv()
-            total = (total + sib_r[k, yy].astype(F32)).astype(BF16)
-            if d == 0:
-                y_r[k, yy] = total
-            else:
-                y_s[k, yy] = total
-                grad_x[k].start_to(yy, pending)
-
-    gat[...] = (att[...] * u_t[...].astype(F32) * live).astype(BF16)
-    gw_out = mm(gat[...], c_all[...].reshape(2048, 512))
+        sib_s[k] = partial(k, 1 - c).astype(BF16)
+        start_sib(sib_grad(k))
+    for k in chunks:
+        total = partial(k, c)
+        sib_grad(k).wait_recv()
+        tot[k] = (total + sib_r[k].astype(F32)).astype(BF16)
+        grad_x[k].start(pending)
+        g_r[k, s] = positions(k, s)[...]
+
+    for k in heads:
+        w2_send[k * n : (k + 1) * n, :, 0:384] = to_rows(mm(g_t[128:512, :], e_all[k].reshape(2048, HW)).T)
+    ev_x.wait_recv()
+    sums = jnp.zeros((512, 256), F32)
+    for blk in range(8):
+        hit = onehot(iota((512, 256), 0) == ev_all[blk, 0:1, :])
+        sums += mm_nt(hit, jnp.concatenate([tot[k, :, blk * 256 : (blk + 1) * 256] for k in chunks], axis=0))
     for b in range(4):
-        w_send[4 * b : 4 * b + 4, :, 512:640] = gw_out[:, b * 128 : (b + 1) * 128].astype(BF16).reshape(4, 32, 128)
-    for k in chunks:
-        gw_in = mm(g_t[...], e_all[k].reshape(2048, CW))
-        n = CW // 32
-        w_send[k * n : (k + 1) * n, :, 0:512] = gw_in.T.astype(BF16).reshape(n, 32, 512)
-    ev_x.wait_recv()
-    for k in chunks:
-        sums = jnp.zeros((512, CW), F32)
-        for yy in range(4):
-            for same in range(2):
-                blk = 2 * yy + (c if same else 1 - c)
-                hit = onehot(iota((512, 256), 0) == ev_all[blk, 0:1, :])
-                sums += mm_nt(hit, (own_p if same else sib_s)[k, yy])
-        for b in range(2):
-            blk = 2 * h + b
-            hit = jnp.logical_and(
-                iota((512, 256), 0) == ev_all[blk, 0:1, :], blk * 256 + iota((1, 256), 1) < len_ref[u]
-            )
-            sums += mm(onehot(hit), c_all[blk, :, k * CW : (k + 1) * CW])
-        w_send[:, :, 640 + k * CW : 640 + (k + 1) * CW] = sums.astype(BF16).reshape(16, 32, CW)
-    w_x.start(pending)
-    w_recv[o] = w_send[o]
+        blk = 4 * lax.rem(y, 2) + b
+        hit = jnp.logical_and(
+            iota((512, 256), 0) == ev_all[blk, 0:1, :], blk * 256 + iota((1, 256), 1) < len_ref[u]
+        )
+        sums += mm(onehot(hit), c_all[blk, :, pl.ds(pl.multiple_of(c * 256, 256), 256)])
+    w2_send[:, :, 384:640] = to_rows(sums)
+    w2_x.start(pending)
+    w2_recv[o] = w2_send[o]
 
     cots = []
     for uu in range(2):
@@ -438,21 +457,28 @@
     hits = jnp.concatenate(hits, axis=1)
     for k in chunks:
         grad_x[k].wait_recv()
-        for uu in range(2):
-            grad[:, uu * 256 : (uu + 1) * 256] = (
-                y_r[k, 2 * uu].astype(F32) + y_r[k, 2 * uu + 1].astype(F32)
-            ).astype(BF16)
-        sums = mm_nt(hits, grad[...]) + mm(hits, cot[:, k * CW : (k + 1) * CW])
-        s_send[k] = sums.astype(BF16).reshape(16, 32, CW)
+        here = []
+        for half in range(2):
+            rows_k = slice(half * HALF, (half + 1) * HALF)
+            for uu in range(2):
+                grad[rows_k, uu * 256 : (uu + 1) * 256] = (
+                    g_r[k, 4 * uu + half].astype(F32) + g_r[k, 4 * uu + 2 + half].astype(F32)
+                ).astype(BF16)
+            here.append(cot[:, half * 256 + k * HALF : half * 256 + (k + 1) * HALF])
+        sums = mm_nt(hits, grad[...]) + mm(hits, jnp.concatenate(here, axis=1))
+        s_send[k] = to_rows(sums)
         ret_x1[k].start(pending)
         q_recv[k, o] = s_send[k, o]
 
-    w_x.wait_recv()
-    total = jnp.sum(w_recv[...].astype(F32), axis=0)
-    wu_s[...] = total[:, 0:640].astype(BF16).reshape(2, 16, 640)
-    for i in range(8):
-        left = 640 + 128 * (i % 4)
-        hu_s[i] = total[16 * (i // 4) : 16 * (i // 4) + 16, left : left + 128].astype(BF16)
+    w1_x.wait_recv()
+    total1 = jnp.sum(w1_recv[...].astype(F32), axis=0)
+    w2_x.wait_recv()
+    total2 = jnp.sum(w2_recv[...].astype(F32), axis=0)
+    total = jnp.concatenate([total1[:, 128:256], total2[:, 0:384], total1[:, 0:128]], axis=1)
+    wu_s[...] = total.astype(BF16).reshape(2, 16, 640)
+    for i in range(4):
+        left = 384 + 128 * (i % 2)
+        hu_s[i] = total2[16 * (i // 2) : 16 * (i // 2) + 16, left : left + 128].astype(BF16)
     wu = pltpu.make_async_remote_copy(
         src_ref=wu_s.at[1 - u],
         dst_ref=wu_r,
@@ -463,15 +489,18 @@
     )
     start_sib(wu)
     hot_x.start(pending)
-    hu_r[s] = hu_s[s]
+    hu_r[y] = hu_s[y]
 
     r = iota((512, 512), 0)
     pick = onehot(iota((512, 512), 1) == (r & 15) * 32 + (r >> 4))
-    for k in chunks:
+
+    def second_hop(k):
         ret_x1[k].wait_recv()
         p_send[k] = mm(pick, q_recv[k].reshape(512, CW)).astype(BF16).reshape(8, 4, 16, CW)
         ret_x2[k].start(pending)
         ret[k, :, s] = p_send[k, s]
+
+    second_hop(0)
 
     place = {"y": y, "x": x, "z": z}
     device = {
@@ -498,12 +527,12 @@
     def last_slab(i, core, p):
         order = AG_ORDERS[i]
         blk = slab(i, core, {order[0]: slice(None), order[1]: slice(None), order[2]: p})
-        return to_sib(blk, blk, 2 + 2 * CHUNKS + i, p)
+        return to_sib(blk, blk, 3 + HEAD + i, p)
 
     gathers = [[gather_x(i, stage) for stage in range(3)] for i in range(3)]
     wu.wait_recv()
     pick_u = u.astype(F32)
-    mine = total[0:16, 0:640] * (1.0 - pick_u) + total[16:32, 0:640] * pick_u + wu_r[...].astype(F32)
+    mine = total[0:16] * (1.0 - pick_u) + total[16:32] * pick_u + wu_r[...].astype(F32)
     mine = mine.astype(BF16)
     ag0[c, y, x, z] = mine[:, 0:256]
     ag1[c, y, x, z] = mine[:, 256:512]
@@ -514,6 +543,8 @@
         [mine[:, 512:640], jnp.sum(hu_r[...].astype(F32), axis=0).astype(BF16)], axis=1
     )
     gathers[2][0].start(pending)
+    for k in range(1, CHUNKS):
+        second_hop(k)
     for stage in range(2):
         for i in range(3):
             gathers[i][stage].wait_recv()
@@ -540,7 +571,6 @@
     for yy in range(4):
         for core in range(2):
             user, head = yy // 2, (yy % 2) * 2 + core
-            seq = 2 * yy + core
             for zz in range(2):
                 top = 32 * zz + 16 * user
                 b0 = a0[core, yy, 0, zz].astype(F32)
@@ -551,11 +581,15 @@
                     gin[top : top + 16, b * 512 + head * 128 : b * 512 + head * 128 + 128] = part
                 low = pl.multiple_of(head * 128 + 32 * (2 * lax.rem(g, 2) + zz) + 16 * user, 16)
                 gout[pl.ds(low, 16), pl.ds(pl.multiple_of(g // 2 * 128, 128), 128)] = b2[:, 0:128]
-                hot_top = 32 * zz + 16 * (seq // 4)
-                ghot[hot_top : hot_top + 16, 128 * (seq % 4) : 128 * (seq % 4) + 128] = b2[:, 128:256]
+                hot_top = 32 * zz + 16 * (yy // 2)
+                left = 256 * core + 128 * (yy % 2)
+                ghot[hot_top : hot_top + 16, left : left + 128] = b2[:, 128:256]
     hits = jnp.concatenate([onehot(iota((256, 128), 0) + g * 256 == asked[i : i + 1, :]) for i in range(4)], axis=1)
     for k in range(CHUNKS):
-        gcold[:, k * CW : (k + 1) * CW] = mm(hits, ret[k].reshape(512, CW))
+        sums = mm(hits, ret[k].reshape(512, CW))
+        for half in range(2):
+            left = half * 256 + k * HALF
+            gcold[:, left : left + HALF] = sums[:, half * HALF : (half + 1) * HALF]
 
 
 def on_device(
@@ -580,12 +614,12 @@
         ints(8, 8, 256),
         ints(512, 128),
         wide(512, 128),
-        big(CHUNKS, 4, 8, 16, CW),
-        big(CHUNKS, 8, 4, 16, CW),
-        big(CHUNKS, 16, 32, CW),
-        big(CHUNKS, 16, 32, CW),
-        big(CHUNKS, 2, 256, CW),
-        big(CHUNKS, 8, 256, CW),
+        big(HEAD, 4, 8, 16, HW),
+        big(HEAD, 8, 4, 16, HW),
+        big(HEAD, 16, 32, HW),
+        big(HEAD, 16, 32, HW),
+        big(HEAD, 2, 256, HW),
+        big(HEAD, 8, 256, HW),
         big(8, 256, 512),
         big(512, 512),
         big(512, 512),
@@ -610,31 +644,37 @@
         wide(2048, 128),
         big(512, 2048),
         wide(4, 4, 2048),
-        big(CHUNKS, 4, CW, 256),
-        big(CHUNKS, 4, CW, 256),
-        big(CHUNKS, 4, CW, 256),
-        big(CHUNKS, 4, CW, 256),
-        big(CHUNKS, 4, CW, 256),
+        big(CHUNKS, HALF, 2048),
+        big(CHUNKS, HALF, 2048),
+        big(CHUNKS, HALF, 2048),
+        big(CHUNKS, 8, HALF, 256),
         big(CW, 512),
-        big(16, 32, 1152),
-        big(16, 32, 1152),
+        big(16, 32, 256),
+        big(16, 32, 256),
+        big(16, 32, 640),
+        big(16, 32, 640),
         big(2, 16, 640),
         big(16, 640),
-        big(8, 16, 128),
-        big(8, 16, 128),
+        big(4, 16, 128),
+        big(4, 16, 128),
         big(CHUNKS, 16, 32, CW),
         big(CHUNKS, 16, 32, CW),
         big(CHUNKS, 8, 4, 16, CW),
-        sems((2 + 2 * CHUNKS, 2, 16)),
-        sems((3 + 2 * CHUNKS, 2, 8)),
-        sems((2 + 2 * CHUNKS, 2, 4)),
+        big(2, 256, 512),
+        big(512, 512),
+        big(512, 512),
+        big(2048, 512),
+        sems((4,)),
+        sems((3 + HEAD + CHUNKS, 2, 16)),
+        sems((2 + HEAD + 2 * CHUNKS, 2, 8)),
+        sems((3 + HEAD, 2, 4)),
         sems((3, 3, 2, 4)),
-        sems((5 + 2 * CHUNKS, 2, 4)),
+        sems((6 + HEAD, 2, 4)),
     ]
     a0, a1, a2, ret, asked = pl.pallas_call(
         main_kernel,
         out_shape=outs,
-        in_specs=[vmem] * 3 + [smem] + [vmem] * 4 + [pl.BlockSpec(memory_space=pl.ANY)],
+        in_specs=[vmem] * 3 + [smem] + [pl.BlockSpec(memory_space=pl.ANY)] * 5,
         out_specs=[vmem] * 5,
         scratch_shapes=scratch,
         compiler_params=pltpu.CompilerParams(

time: 145 us -> 129 us (0.89)
  Pallas kernels: 145 us -> 128 us
    pallas_call x1, Pallas kernels: 136 us -> 120 us  [on_device(): pl.pallas_call(main_kernel, out_shape=outs, in_specs=[vmem] * 3 + [smem]...]
where the time goes in v3:
time: 129 us
  Pallas kernels  128 us (99%)
    pallas_call x1, Pallas kernels, on_device(): pl.pallas_call(main_kernel, out_shape=outs, in_specs=[vmem] * 3 + [smem]...  120 us
    pallas_call x1, Pallas kernels, on_device(): pl.pallas_call(finish_kernel, grid=(8,), out_shape=[jax.ShapeDtypeStruct(...  8.79 us

profile of v3, /device:TPU:1, one launch (start us, length us, event | category | flops | bytes accessed | tf_op | source)
XLA Modules:
  0.0 129.1 jit_solution(6657597981228884289)
XLA Ops:
  0.6 119.7 %layer.1 = (bf16[2,4,4,4,16,256]{5,4,3,2,1,0:T(8,128)(2,1)}, bf16[2,4,4,4,16,256]{5,4,3,2,1,0:T(8,128)(2,1)}, bf16[2,4,4,4,16,256]{5,4,3,2,1,0:T(8,128)(2,1)}, b...) custom-call(s32[4,128]{1,0:T(4,128)} %bitcast.2, s32[1,128]{1,0:T(1,128)} %bitcast.3, s32[2,256]{1,0:T(2,128)} %ev_ref.1, ...), custom_call_target="tpu_custom_call" | custom-call | tf_op jit(solution)/shard_map/layer/pallas_call | solution.py:674
  120.4 8.8 %finish.1 = (f32[512,2048]{1,0:T(8,128)}, f32[512,512]{1,0:T(8,128)}, f32[512,512]{1,0:T(8,128)}, f32[2048,512]{1,0:T(8,128)}) custom-call(bf16[2,4,4,4,16,256]{5,4,3,2,1,0:T(8,128)(2,1)} %get-tuple-element.9.a0, bf16[2,4,4,4,16,256]{5,4,3,2,1,0:T(8,128)(2,1)} %get-tuple-element.10.a1, bf16[2,4,4,4,16,256]{5,4,3,2,1,0:T(8,128)(2,1)} %get-tuple-element.11.a2, ...), custom_call_target="tpu_custom_call" | custom-call | tf_op jit(solution)/shard_map/finish/pallas_call | solution.py:690

commit v4 on v3

--- a/solution.py
+++ b/solution.py
@@ -35,6 +35,25 @@
     return hit.astype(F32).astype(BF16)
 
 
+def hops(step):
+    return sum(min(d, 4 - d) for d in step[:2])
+
+
+STEPS = {
+    4: [(2,), (1,), (3,)],
+    16: sorted(((dx, dz) for dx in range(4) for dz in range(4) if dx or dz), key=hops, reverse=True),
+    8: [(2, 0), (2, 1), (1, 0), (1, 1), (3, 0), (3, 1), (0, 1)],
+}
+
+
+def away(n, me, step):
+    if n == 4:
+        return lax.rem(me + step[0], 4)
+    if n == 16:
+        return lax.rem(me // 4 + step[0], 4) * 4 + lax.rem(lax.rem(me, 4) + step[1], 4)
+    return lax.rem(me // 2 + step[0], 4) * 2 + lax.rem(lax.rem(me, 2) + step[1], 2)
+
+
 class Exchange:
     def __init__(self, n, me, device, src, dst, send_sem, recv_sem):
         self.n, self.me, self.device, self.src, self.dst = n, me, device, src, dst
@@ -60,15 +79,13 @@
             device_id_type=MESH,
         )
 
-    def peer(self, k):
-        return lax.rem(self.me + k, self.n)
-
-    def _each(self, f):
-        if self.n <= 16:
-            for k in range(1, self.n):
-                f(self.peer(k))
-        else:
-            pl.loop(1, self.n)(lambda k: f(self.peer(k)))
+    def peers(self):
+        return [away(self.n, self.me, step) for step in STEPS[self.n]]
+
+    def _each(self, f, near_first=False):
+        peers = self.peers()
+        for p in peers[::-1] if near_first else peers:
+            f(p)
 
     def start(self, pending):
         pending.append(self.wait_send)
@@ -82,7 +99,7 @@
         self._in(p).wait_recv()
 
     def wait_recv(self):
-        self._each(lambda p: self._in(p).wait_recv())
+        self._each(lambda p: self._in(p).wait_recv(), near_first=True)
 
     def wait_send(self):
         self._each(lambda p: self._out(p).wait_send())
@@ -111,13 +128,10 @@
 
     barrier = pltpu.get_barrier_semaphore()
 
-    @pl.loop(1, 16)
-    def _(k):
-        pl.semaphore_signal(barrier, inc=1, device_id=(s, lax.rem(o + k, 16)), device_id_type=MESH)
-
-    @pl.loop(1, 8)
-    def _(k):
-        pl.semaphore_signal(barrier, inc=1, device_id=(lax.rem(s + k, 8), o), device_id_type=MESH)
+    for step in STEPS[16]:
+        pl.semaphore_signal(barrier, inc=1, device_id=(s, away(16, o, step)), device_id_type=MESH)
+    for step in STEPS[8]:
+        pl.semaphore_signal(barrier, inc=1, device_id=(away(8, s, step), o), device_id_type=MESH)
 
     def load_w(b):
         return pltpu.make_async_copy(
@@ -317,7 +331,7 @@
             t = jnp.tanh(half)
             a = 1.0 + t
             w = half * a
-            slope = a * ((1.0 + 2.0 * half) - w)
+            slope = a + w * (2.0 - a)
             if diag:
                 ok = iota((128, 512), 0) + m * 128 <= iota((128, 512), 1)
                 w = jnp.where(ok, w, 0.0)
@@ -455,7 +469,7 @@
         hit = iota((512, 256), 0) + 512 == ev_loc[uu, 0:1, :]
         hits.append(onehot(jnp.logical_and(hit, jnp.concatenate([valid_col[...]] * 2, axis=1) > 0)))
     hits = jnp.concatenate(hits, axis=1)
-    for k in chunks:
+    def first_hop(k):
         grad_x[k].wait_recv()
         here = []
         for half in range(2):
@@ -469,6 +483,8 @@
         s_send[k] = to_rows(sums)
         ret_x1[k].start(pending)
         q_recv[k, o] = s_send[k, o]
+
+    first_hop(0)
 
     w1_x.wait_recv()
     total1 = jnp.sum(w1_recv[...].astype(F32), axis=0)
@@ -490,6 +506,8 @@
     start_sib(wu)
     hot_x.start(pending)
     hu_r[y] = hu_s[y]
+    for k in range(1, CHUNKS):
+        first_hop(k)
 
     r = iota((512, 512), 0)
     pick = onehot(iota((512, 512), 1) == (r & 15) * 32 + (r >> 4))
@@ -499,8 +517,6 @@
         p_send[k] = mm(pick, q_recv[k].reshape(512, CW)).astype(BF16).reshape(8, 4, 16, CW)
         ret_x2[k].start(pending)
         ret[k, :, s] = p_send[k, s]
-
-    second_hop(0)
 
     place = {"y": y, "x": x, "z": z}
     device = {
@@ -543,12 +559,14 @@
         [mine[:, 512:640], jnp.sum(hu_r[...].astype(F32), axis=0).astype(BF16)], axis=1
     )
     gathers[2][0].start(pending)
-    for k in range(1, CHUNKS):
-        second_hop(k)
+    second_hop(0)
     for stage in range(2):
         for i in range(3):
             gathers[i][stage].wait_recv()
             gathers[i][stage + 1].start(pending)
+        if stage == 0:
+            for k in range(1, CHUNKS):
+                second_hop(k)
     for i in range(3):
         start_sib(last_slab(i, c, place[AG_ORDERS[i][2]]))
     for d in (1, 3, 2):
@@ -600,9 +618,9 @@
     big = lambda *shape: pltpu.VMEM(shape, BF16)
     wide = lambda *shape: pltpu.VMEM(shape, F32)
     sems = pltpu.SemaphoreType.DMA
-    outs = [jax.ShapeDtypeStruct((2, 4, 4, 4, 16, 256), BF16)] * 3 + [
-        jax.ShapeDtypeStruct((CHUNKS, 4, 8, 16, CW), BF16),
-        jax.ShapeDtypeStruct((8, 128), jnp.int32),
+    outs = [pltpu.VMEM((2, 4, 4, 4, 16, 256), BF16)] * 3 + [
+        pltpu.VMEM((CHUNKS, 4, 8, 16, CW), BF16),
+        pltpu.VMEM((8, 128), jnp.int32),
     ]
     ints = lambda *shape: pltpu.VMEM(shape, jnp.int32)
     scratch = [
@@ -678,7 +696,7 @@
         out_specs=[vmem] * 5,
         scratch_shapes=scratch,
         compiler_params=pltpu.CompilerParams(
-            collective_id=0, has_side_effects=True, vmem_limit_bytes=60 * 1024 * 1024
+            collective_id=0, has_side_effects=True, vmem_limit_bytes=56 * 1024 * 1024
         ),
         name="layer",
     )(
@@ -707,7 +725,7 @@
             pl.BlockSpec((64, 512), lambda g: (g, 0)),
             pl.BlockSpec((256, 512), lambda g: (g, 0)),
         ],
-        compiler_params=pltpu.CompilerParams(vmem_limit_bytes=60 * 1024 * 1024),
+        compiler_params=pltpu.CompilerParams(vmem_limit_bytes=24 * 1024 * 1024),
         name="finish",
     )(a0, a1, a2, ret, asked)
 

time: 129 us -> 122 us (0.946)
  Pallas kernels: 128 us -> 121 us
    pallas_call x1, Pallas kernels: 120 us -> 115 us  [on_device(): pl.pallas_call(main_kernel, out_shape=outs, in_specs=[vmem] * 3 + [smem]...]
    pallas_call x1, Pallas kernels: 8.79 us -> 5.94 us  [on_device(): pl.pallas_call(finish_kernel, grid=(8,), out_shape=[jax.ShapeDtypeStruct(...]
where the time goes in v4:
time: 122 us
  Pallas kernels  121 us (99%)
    pallas_call x1, Pallas kernels, on_device(): pl.pallas_call(main_kernel, out_shape=outs, in_specs=[vmem] * 3 + [smem]...  115 us
    pallas_call x1, Pallas kernels, on_device(): pl.pallas_call(finish_kernel, grid=(8,), out_shape=[jax.ShapeDtypeStruct(...  5.94 us

profile of v4, /device:TPU:1, one launch (start us, length us, event | category | flops | bytes accessed | tf_op | source)
XLA Modules:
  0.0 121.9 jit_solution(6307853030722790382)
XLA Ops:
  0.6 115.3 %layer.1 = (bf16[2,4,4,4,16,256]{5,4,3,2,1,0:T(8,128)(2,1)S(1)}, bf16[2,4,4,4,16,256]{5,4,3,2,1,0:T(8,128)(2,1)S(1)}, bf16[2,4,4,4,16,256]{5,4,3,2,1,0:T(8,128)(...) custom-call(s32[4,128]{1,0:T(4,128)} %bitcast.2, s32[1,128]{1,0:T(1,128)} %bitcast.3, s32[2,256]{1,0:T(2,128)} %ev_ref.1, ...), custom_call_target="tpu_custom_call" | custom-call | tf_op jit(solution)/shard_map/layer/pallas_call | solution.py:692
  115.9 5.9 %finish.1 = (f32[512,2048]{1,0:T(8,128)}, f32[512,512]{1,0:T(8,128)}, f32[512,512]{1,0:T(8,128)}, f32[2048,512]{1,0:T(8,128)}) custom-call(bf16[2,4,4,4,16,256]{5,4,3,2,1,0:T(8,128)(2,1)S(1)} %get-tuple-element.9.a0, bf16[2,4,4,4,16,256]{5,4,3,2,1,0:T(8,128)(2,1)S(1)} %get-tuple-element.10.a1, bf16[2,4,4,4,16,256]{5,4,3,2,1,0:T(8,128)(2,1)S(1)} %get-tuple-element.11.a2, ...), custom_call_target="tpu_custom_call" | custom-call | tf_op jit(solution)/shard_map/finish/pallas_call | solution.py:708

commit v5 on v4

--- a/solution.py
+++ b/solution.py
@@ -112,7 +112,7 @@
     got, rows, perm, fetched, e_loc, e_all, c_all,
     wh, wht, wh_sem, slope_pre, u_t, q_t, k_t, v_t, q_n, k_n, v_n,
     w_st, sl_st, att, gg, gat, ga_t, ga_n, gq, gk, gv, g_t, stat,
-    sib_s, sib_r, tot, g_r, grad, w1_send, w1_recv, w2_send, w2_recv, wu_s, wu_r, hu_s, hu_r,
+    hot_hit, hot_acc, sib_s, sib_r, tot, g_r, grad, w1_send, w1_recv, w2_send, w2_recv, wu_s, wu_r, hu_s, hu_r,
     s_send, q_recv, p_send, dout_ref, wout_ref, hot_ref, table_ref, load_sem,
     sem16, sem8, sem4, sem_ag, sem_sib,
 ):
@@ -143,7 +143,7 @@
     loads = [
         pltpu.make_async_copy(a, b, load_sem.at[i])
         for i, (a, b) in enumerate(
-            ((table_any, table_ref), (dout_any, dout_ref), (hot_any, hot_ref), (wout_any, wout_ref))
+            ((dout_any, dout_ref), (table_any, table_ref), (hot_any, hot_ref), (wout_any, wout_ref))
         )
     ]
     for copy in loads:
@@ -214,6 +214,8 @@
 
     ids_x1.start(pending)
     id_a[o] = id_loc[:, o, :]
+    loads[0].wait()
+    cot_x.start_to(lax.rem(y + 2, 4), pending)
 
     codes = []
     for uu in range(2):
@@ -237,7 +239,7 @@
     for b in range(4):
         load_w(b).wait()
     wht[...] = wh[...].T
-    for copy in loads:
+    for copy in loads[1:]:
         copy.wait()
     c_all[s] = dout_ref[u]
 
@@ -270,6 +272,8 @@
         fetched[k, o] = perm[k, o]
     for d in (1, 3):
         cot_x.start_to(lax.rem(y + d, 4), pending)
+    cot_x.wait_from(lax.rem(y + 2, 4))
+    start_sib(sib_block(c_all, 0, lax.rem(y + 2, 4)))
     cold_hits = [
         onehot(jnp.logical_and(
             code_col[...] == iota((512, 128), 1) + (512 + b * 128), valid_row[:, b * 128 : (b + 1) * 128]
@@ -305,20 +309,42 @@
     for d in (1, 3):
         cot_x.wait_from(lax.rem(y + d, 4))
         start_sib(sib_block(c_all, 0, lax.rem(y + d, 4)))
-    project(s)
-    for k in heads:
-        for d in (1, 3, 2):
-            yy = lax.rem(y + d, 4)
-            emb_x[k].wait_from(yy)
-            start_sib(sib_block(e_all.at[k], 2 + k, yy))
-            if k == HEAD - 1:
-                project(2 * yy + c)
-    cot_x.start_to(lax.rem(y + 2, 4), pending)
-    for d in (0, 1, 3, 2):
+    def arrive(k, d):
+        yy = lax.rem(y + d, 4)
+        emb_x[k].wait_from(yy)
+        start_sib(sib_block(e_all.at[k], 2 + k, yy))
+
+    def project_sib(d):
         yy = lax.rem(y + d, 4)
         for k in heads:
             sib_block_in(e_all.at[k], 2 + k, yy).wait_recv()
         project(2 * yy + 1 - c)
+
+    live = (iota((1, 2048), 1) < len_ref[u]).astype(F32)
+
+    def gate_grad(blk):
+        cols = pl.ds(pl.multiple_of(blk * 256, 256), 256)
+        here = (blk * 256 + iota((1, 256), 1) < len_ref[u]).astype(F32)
+        wo = wout_ref[pl.ds(pl.multiple_of(h * 128, 128), 128), :]
+        gg[:, cols] = mm_nt(wo, c_all[blk]) * here
+
+    project(s)
+    for k in range(HEAD - 1):
+        for d in (1, 3, 2):
+            arrive(k, d)
+    for d in (0, 2, 1, 3):
+        yy = lax.rem(y + d, 4)
+        sib_block_in(c_all, 0, yy).wait_recv()
+        gate_grad(2 * yy + c)
+        gate_grad(2 * yy + 1 - c)
+    for d in (1, 3):
+        arrive(HEAD - 1, d)
+        project(2 * lax.rem(y + d, 4) + c)
+    for d in (0, 1, 3):
+        project_sib(d)
+    arrive(HEAD - 1, 2)
+    project(2 * lax.rem(y + 2, 4) + c)
+    project_sib(2)
 
     att[...] = jnp.zeros_like(att)
 
@@ -348,13 +374,6 @@
 
         forward(i, i, True)
 
-    cot_x.wait_from(lax.rem(y + 2, 4))
-    start_sib(sib_block(c_all, 0, lax.rem(y + 2, 4)))
-    for d in range(4):
-        sib_block_in(c_all, 0, lax.rem(y + d, 4)).wait_recv()
-    live = (iota((1, 2048), 1) < len_ref[u]).astype(F32)
-    wo = wout_ref[pl.ds(pl.multiple_of(h * 128, 128), 128), :]
-    gg[...] = mm_nt(wo, c_all[...].reshape(2048, 512)) * live
     inv = 1.0 / jnp.full((1, 2048), len_ref[u], jnp.int32).astype(F32)
     mine = att[...] * inv
     m1 = jnp.sum(mine, axis=0, keepdims=True) * (1.0 / 128)
@@ -365,6 +384,17 @@
     stat[h, 2:3, :] = jnp.sum(gn, axis=0, keepdims=True)
     stat[h, 3:4, :] = jnp.sum(gn * dev, axis=0, keepdims=True)
     stat_x.start(pending)
+    ev_x.wait_recv()
+    for blk in range(8):
+        hot_hit[:, blk * 256 : (blk + 1) * 256] = onehot(iota((512, 256), 0) == ev_all[blk, 0:1, :])
+    part = pl.ds(pl.multiple_of(c * 256, 256), 256)
+    sums = jnp.zeros((512, 256), F32)
+    for b in range(4):
+        blk = 4 * lax.rem(y, 2) + b
+        here = (blk * 256 + iota((256, 1), 0) < len_ref[u]).astype(F32)
+        kept = (c_all[blk, :, part].astype(F32) * here).astype(BF16)
+        sums += mm(hot_hit[:, pl.ds(pl.multiple_of(blk * 256, 256), 256)], kept)
+    hot_acc[...] = sums
     stat_x.wait_recv()
     both = stat[...]
     mean = jnp.sum(both[:, 0, :], axis=0, keepdims=True) * 0.25
@@ -435,6 +465,8 @@
     for k in chunks:
         sib_s[k] = partial(k, 1 - c).astype(BF16)
         start_sib(sib_grad(k))
+    for k in heads:
+        w2_send[k * n : (k + 1) * n, :, 0:384] = to_rows(mm(g_t[128:512, :], e_all[k].reshape(2048, HW)).T)
     for k in chunks:
         total = partial(k, c)
         sib_grad(k).wait_recv()
@@ -442,19 +474,7 @@
         grad_x[k].start(pending)
         g_r[k, s] = positions(k, s)[...]
 
-    for k in heads:
-        w2_send[k * n : (k + 1) * n, :, 0:384] = to_rows(mm(g_t[128:512, :], e_all[k].reshape(2048, HW)).T)
-    ev_x.wait_recv()
-    sums = jnp.zeros((512, 256), F32)
-    for blk in range(8):
-        hit = onehot(iota((512, 256), 0) == ev_all[blk, 0:1, :])
-        sums += mm_nt(hit, jnp.concatenate([tot[k, :, blk * 256 : (blk + 1) * 256] for k in chunks], axis=0))
-    for b in range(4):
-        blk = 4 * lax.rem(y, 2) + b
-        hit = jnp.logical_and(
-            iota((512, 256), 0) == ev_all[blk, 0:1, :], blk * 256 + iota((1, 256), 1) < len_ref[u]
-        )
-        sums += mm(onehot(hit), c_all[blk, :, pl.ds(pl.multiple_of(c * 256, 256), 256)])
+    sums = hot_acc[...] + mm_nt(hot_hit[...], tot[...].reshape(256, 2048))
     w2_send[:, :, 384:640] = to_rows(sums)
     w2_x.start(pending)
     w2_recv[o] = w2_send[o]
@@ -662,6 +682,8 @@
         wide(2048, 128),
         big(512, 2048),
         wide(4, 4, 2048),
+        big(512, 2048),
+        wide(512, 256),
         big(CHUNKS, HALF, 2048),
         big(CHUNKS, HALF, 2048),
         big(CHUNKS, HALF, 2048),

time: 122 us -> 119 us (0.975)
  Pallas kernels: 121 us -> 118 us
    pallas_call x1, Pallas kernels: 115 us -> 113 us  [on_device(): pl.pallas_call(main_kernel, out_shape=outs, in_specs=[vmem] * 3 + [smem]...]
where the time goes in v5:
time: 119 us
  Pallas kernels  118 us (99%)
    pallas_call x1, Pallas kernels, on_device(): pl.pallas_call(main_kernel, out_shape=outs, in_specs=[vmem] * 3 + [smem]...  113 us
    pallas_call x1, Pallas kernels, on_device(): pl.pallas_call(finish_kernel, grid=(8,), out_shape=[jax.ShapeDtypeStruct(...  5.94 us

profile of v5, /device:TPU:1, one launch (start us, length us, event | category | flops | bytes accessed | tf_op | source)
XLA Modules:
  0.0 119.2 jit_solution(6107570490068216909)
XLA Ops:
  0.6 112.6 %layer.1 = (bf16[2,4,4,4,16,256]{5,4,3,2,1,0:T(8,128)(2,1)S(1)}, bf16[2,4,4,4,16,256]{5,4,3,2,1,0:T(8,128)(2,1)S(1)}, bf16[2,4,4,4,16,256]{5,4,3,2,1,0:T(8,128)(...) custom-call(s32[4,128]{1,0:T(4,128)} %bitcast.2, s32[1,128]{1,0:T(1,128)} %bitcast.3, s32[2,256]{1,0:T(2,128)} %ev_ref.1, ...), custom_call_target="tpu_custom_call" | custom-call | tf_op jit(solution)/shard_map/layer/pallas_call | solution.py:714
  113.2 5.9 %finish.1 = (f32[512,2048]{1,0:T(8,128)}, f32[512,512]{1,0:T(8,128)}, f32[512,512]{1,0:T(8,128)}, f32[2048,512]{1,0:T(8,128)}) custom-call(bf16[2,4,4,4,16,256]{5,4,3,2,1,0:T(8,128)(2,1)S(1)} %get-tuple-element.9.a0, bf16[2,4,4,4,16,256]{5,4,3,2,1,0:T(8,128)(2,1)S(1)} %get-tuple-element.10.a1, bf16[2,4,4,4,16,256]{5,4,3,2,1,0:T(8,128)(2,1)S(1)} %get-tuple-element.11.a2, ...), custom_call_target="tpu_custom_call" | custom-call | tf_op jit(solution)/shard_map/finish/pallas_call | solution.py:730

commit v6 on v5

--- a/solution.py
+++ b/solution.py
@@ -456,6 +456,9 @@
         g_t[256:384, cols] = (gk[cols, :].T * (0.5 * SCALE) * slope_pre[256:384, cols]).astype(BF16)
         g_t[384:512, cols] = (gv[cols, :].T * keep[:, cols] * slope_pre[384:512, cols]).astype(BF16)
 
+    head_sends = list(pending)
+    pending.clear()
+
     def partial(k, half):
         return mm(wh[pl.ds(pl.multiple_of(half * 256 + k * HALF, HALF), HALF), :], g_t[...])
 
@@ -465,19 +468,24 @@
     for k in chunks:
         sib_s[k] = partial(k, 1 - c).astype(BF16)
         start_sib(sib_grad(k))
-    for k in heads:
-        w2_send[k * n : (k + 1) * n, :, 0:384] = to_rows(mm(g_t[128:512, :], e_all[k].reshape(2048, HW)).T)
     for k in chunks:
         total = partial(k, c)
         sib_grad(k).wait_recv()
         tot[k] = (total + sib_r[k].astype(F32)).astype(BF16)
         grad_x[k].start(pending)
         g_r[k, s] = positions(k, s)[...]
+        if k == 0:
+            for b in heads:
+                w2_send[b * n : (b + 1) * n, :, 0:384] = to_rows(mm(g_t[128:512, :], e_all[b].reshape(2048, HW)).T)
 
     sums = hot_acc[...] + mm_nt(hot_hit[...], tot[...].reshape(256, 2048))
     w2_send[:, :, 384:640] = to_rows(sums)
     w2_x.start(pending)
     w2_recv[o] = w2_send[o]
+    for wait in head_sends:
+        wait()
+    grad_sends = list(pending)
+    pending.clear()
 
     cots = []
     for uu in range(2):
@@ -579,6 +587,10 @@
         [mine[:, 512:640], jnp.sum(hu_r[...].astype(F32), axis=0).astype(BF16)], axis=1
     )
     gathers[2][0].start(pending)
+    for wait in grad_sends:
+        wait()
+    hop_sends = list(pending)
+    pending.clear()
     second_hop(0)
     for stage in range(2):
         for i in range(3):
@@ -589,6 +601,8 @@
                 second_hop(k)
     for i in range(3):
         start_sib(last_slab(i, c, place[AG_ORDERS[i][2]]))
+    for wait in hop_sends:
+        wait()
     for d in (1, 3, 2):
         for i in range(3):
             p = lax.rem(place[AG_ORDERS[i][2]] + d, 4)
@@ -609,7 +623,7 @@
     for yy in range(4):
         for core in range(2):
             user, head = yy // 2, (yy % 2) * 2 + core
-            for zz in range(2):
+            for zz in range(4):
                 top = 32 * zz + 16 * user
                 b0 = a0[core, yy, 0, zz].astype(F32)
                 b1 = a1[core, yy, 0, zz].astype(F32)
@@ -617,12 +631,12 @@
                 for b in range(4):
                     part = (b0, b1)[b // 2][:, (b % 2) * 128 : (b % 2) * 128 + 128]
                     gin[top : top + 16, b * 512 + head * 128 : b * 512 + head * 128 + 128] = part
-                low = pl.multiple_of(head * 128 + 32 * (2 * lax.rem(g, 2) + zz) + 16 * user, 16)
-                gout[pl.ds(low, 16), pl.ds(pl.multiple_of(g // 2 * 128, 128), 128)] = b2[:, 0:128]
+                low = head * 128 + 32 * zz + 16 * user
+                gout[low : low + 16, pl.ds(pl.multiple_of(g * 128, 128), 128)] = b2[:, 0:128]
                 hot_top = 32 * zz + 16 * (yy // 2)
                 left = 256 * core + 128 * (yy % 2)
                 ghot[hot_top : hot_top + 16, left : left + 128] = b2[:, 128:256]
-    hits = jnp.concatenate([onehot(iota((256, 128), 0) + g * 256 == asked[i : i + 1, :]) for i in range(4)], axis=1)
+    hits = jnp.concatenate([onehot(iota((512, 128), 0) + g * 512 == asked[i : i + 1, :]) for i in range(4)], axis=1)
     for k in range(CHUNKS):
         sums = mm(hits, ret[k].reshape(512, CW))
         for half in range(2):
@@ -726,10 +740,10 @@
         d_out, weight_out, hot_table, cold_table, weight_in,
     )
 
-    part = pl.BlockSpec((2, 4, 1, 2, 16, 256), lambda g: (0, 0, g // 2, lax.rem(g, 2), 0, 0))
+    part = pl.BlockSpec((2, 4, 1, 4, 16, 256), lambda g: (0, 0, g, 0, 0, 0))
     return pl.pallas_call(
         finish_kernel,
-        grid=(8,),
+        grid=(4,),
         out_shape=[
             jax.ShapeDtypeStruct((512, 2048), F32),
             jax.ShapeDtypeStruct((512, 512), F32),
@@ -742,10 +756,10 @@
             pl.BlockSpec((8, 128), lambda g: (0, 0)),
         ],
         out_specs=[
-            pl.BlockSpec((64, 2048), lambda g: (g, 0)),
+            pl.BlockSpec((128, 2048), lambda g: (g, 0)),
             pl.BlockSpec((512, 512), lambda g: (0, 0)),
-            pl.BlockSpec((64, 512), lambda g: (g, 0)),
-            pl.BlockSpec((256, 512), lambda g: (g, 0)),
+            pl.BlockSpec((128, 512), lambda g: (g, 0)),
+            pl.BlockSpec((512, 512), lambda g: (g, 0)),
         ],
         compiler_params=pltpu.CompilerParams(vmem_limit_bytes=24 * 1024 * 1024),
         name="finish",

time: 119 us -> 118 us (level)
  no operation moved by 1% of the time
where the time goes in v6:
time: 118 us
  Pallas kernels  117 us (99%)
    pallas_call x1, Pallas kernels, on_device(): pl.pallas_call(main_kernel, out_shape=outs, in_specs=[vmem] * 3 + [smem]...  113 us
    pallas_call x1, Pallas kernels, on_device(): pl.pallas_call(finish_kernel, grid=(4,), out_shape=[jax.ShapeDtypeStruct(...  4.9 us

profile of v6, /device:TPU:1, one launch (start us, length us, event | category | flops | bytes accessed | tf_op | source)
XLA Modules:
  0.0 118.1 jit_solution(16904096708555303264)
XLA Ops:
  0.6 112.6 %layer.1 = (bf16[2,4,4,4,16,256]{5,4,3,2,1,0:T(8,128)(2,1)S(1)}, bf16[2,4,4,4,16,256]{5,4,3,2,1,0:T(8,128)(2,1)S(1)}, bf16[2,4,4,4,16,256]{5,4,3,2,1,0:T(8,128)(...) custom-call(s32[4,128]{1,0:T(4,128)} %bitcast.2, s32[1,128]{1,0:T(1,128)} %bitcast.3, s32[2,256]{1,0:T(2,128)} %ev_ref.1, ...), custom_call_target="tpu_custom_call" | custom-call | tf_op jit(solution)/shard_map/layer/pallas_call | solution.py:728
  113.2 4.9 %finish.1 = (f32[512,2048]{1,0:T(8,128)}, f32[512,512]{1,0:T(8,128)}, f32[512,512]{1,0:T(8,128)}, f32[2048,512]{1,0:T(8,128)}) custom-call(bf16[2,4,4,4,16,256]{5,4,3,2,1,0:T(8,128)(2,1)S(1)} %get-tuple-element.9.a0, bf16[2,4,4,4,16,256]{5,4,3,2,1,0:T(8,128)(2,1)S(1)} %get-tuple-element.10.a1, bf16[2,4,4,4,16,256]{5,4,3,2,1,0:T(8,128)(2,1)S(1)} %get-tuple-element.11.a2, ...), custom_call_target="tpu_custom_call" | custom-call | tf_op jit(solution)/shard_map/finish/pallas_call | solution.py:744
